TPU v7x, 512 devices: a whole 4x8x8 slice. The times are simulated.
512 devices in a mesh: angle: 64 (over y, z), cuts: 8 (over x, core).
Axes of the slice: x: 4, y: 8, z: 8, core: 2. Of those that a mesh axis runs over, the one named last changes fastest.
Arguments:
- sinogram: bfloat16 [8, 768, 4096], P('cuts', 'angle'), may hold values from -6 to 6
- estimate: bfloat16 [8, 128, 4096], P('cuts', 'angle'), may hold values from -6 to 6
- interp_bank: float32 [4, 128, 64], replicated, may hold values from -0.05 to 0.95
- interp_index: int32 [128], replicated, may hold values from 0 to 3
- slice_taps: float32 [3], replicated, may hold values from 0.3 to 1
Outputs:
- updated: float32 [8, 128, 4096], P('cuts', 'angle')
Inputs may be any that keep to these rules, and one draw needn't show every extreme that they name: `interp_index`: entries 0 and 1 are not read.
All inputs are finite; a program needn't handle non-finite values.
Results may differ from a plain program's by a relative error of at most 0.0003.
Values sent between devices are 32-bit elements; how exact they have to be, the bound alone decides.
A program may use at most 64 MiB of HBM per device.

v0:
```python
import math

import jax
import jax.numpy as jnp
from jax import lax
from jax.sharding import PartitionSpec as P


def partner_2(value, axis, bit):
    mask = 2**bit
    pairs = [(source, source ^ mask) for source in range(lax.axis_size(axis))]
    return lax.ppermute(value, axis, pairs)


def padded_2(cells, sides, width):
    for axis, dim in sides:
        count = lax.axis_size(axis)
        ends = count - 1
        head = lax.slice_in_dim(cells, 0, width, axis=dim)
        tail = lax.slice_in_dim(cells, cells.shape[dim] - width, cells.shape[dim], axis=dim)
        cells = jnp.concatenate(
            [
                lax.ppermute(tail, axis, [(i, (i + 1) % count) for i in range(ends)]),
                cells,
                lax.ppermute(head, axis, [((i + 1) % count, i) for i in range(ends)]),
            ],
            axis=dim,
        )
    return cells


def leaf_image(sino_group, group_id, group_count, leaf_rows):
    view_count, columns = sino_group.shape
    views_total = view_count * group_count
    margin = leaf_rows * group_count // 4 + 1
    padded_views = jnp.pad(sino_group.astype(jnp.float32), ((0, 0), (margin, margin)))
    row_terms = [(2 * row_pos + 1 - leaf_rows) * group_count for row_pos in range(leaf_rows)]

    def add_view(view_pos, totals):
        view_id = group_id * view_count + view_pos
        view_term = 2 * view_id + 1 - views_total
        rows_out = []
        for row_pos in range(leaf_rows):
            shift_now = row_terms[row_pos] * view_term // (4 * views_total)
            start = margin - shift_now
            piece = lax.dynamic_slice(
                padded_views, (view_pos.astype(jnp.int32), start), (1, columns)
            )
            rows_out.append(piece)
        return totals + jnp.concatenate(rows_out, axis=0)

    summed = lax.fori_loop(0, view_count, add_view, jnp.zeros((leaf_rows, columns), jnp.float32))
    return summed * (1.0 / math.sqrt(view_count))


def matrix(interp_bank, interp_index, heap_node, sub_rows):
    kind_id = interp_index[heap_node]
    return lax.dynamic_slice(interp_bank, (kind_id, 0, 0), (1, 2 * sub_rows, sub_rows))[0]


def refine(interp_bank, interp_index, heap_node, sub_rows, own_part, partner):
    joined = jnp.concatenate(
        [
            matrix(interp_bank, interp_index, heap_node, sub_rows),
            matrix(interp_bank, interp_index, heap_node ^ 1, sub_rows),
        ],
        axis=1,
    )
    stacked = jnp.concatenate([own_part, partner], axis=0)
    if 2 * sub_rows <= 16:
        return jnp.sum(joined[:, :, None] * stacked[None], axis=1)
    return jnp.dot(joined, stacked, precision=lax.Precision.HIGHEST)


def shards(sinogram, estimate, interp_bank, interp_index, slice_taps):
    groups = lax.axis_size("angle")
    group_id = lax.axis_index("angle")
    levels = groups.bit_length() - 1
    sino_slice = sinogram[0]
    leaf_rows = estimate.shape[1]
    sub_image = leaf_image(sino_slice, group_id, groups, leaf_rows)
    for tree_level in range(levels):
        sub_rows = leaf_rows << tree_level
        heap_node = (groups >> tree_level) + (group_id >> tree_level)
        partner = partner_2(sub_image, "angle", tree_level)
        sub_image = refine(interp_bank, interp_index, heap_node, sub_rows, sub_image, partner)
    row_band = lax.dynamic_slice_in_dim(sub_image, group_id * leaf_rows, leaf_rows, 0)
    padded = padded_2(row_band[None], (("cuts", 0),), 1)
    mixed = slice_taps[0] * padded[0] + slice_taps[1] * padded[1] + slice_taps[2] * padded[2]
    return (estimate[0].astype(jnp.float32) - mixed)[None]


def solution(mesh):
    in_specs = (P("cuts", "angle", None), P("cuts", "angle", None), P(), P(), P())
    out_specs = P("cuts", "angle", None)
    return jax.shard_map(shards, mesh=mesh, in_specs=in_specs, out_specs=out_specs, check_vma=False)
```

profile of v0, /device:TPU:1, one launch (start us, length us, event | category | flops | bytes accessed | tf_op | source)
XLA Modules:
  0.0 147.1 jit_solution(4550276214770070862)
XLA Ops:
  0.0 0.0 copy-start
  0.0 1.0 pad_convert_fusion
  1.1 3.4 %while.19 = (s32[]{:T(128)}, f32[2,4096]{1,0:T(2,128)S(1)}, s32[]{:T(128)}, f32[12,4162]{1,0:T(8,128)S(1)}, s32[]{:T(128)}, /*index=5*/s32[]{:T(128)}, s32[]{:T(...) while((s32[]{:T(128)}, f32[2,4096]{1,0:T(2,128)S(1)}, ...), condition=%wide.region_1.2_spmd.clone, body=%wide.region_0.1_spmd.clone.sunk | while | flops 24608 | bytes 164303 | solution.py:52
  1.1 0.1 fusion.33
  1.3 0.1 maximum_add_fusion.2
  1.4 0.1 fusion.33
  1.6 0.1 maximum_add_fusion.2
  1.7 0.1 fusion.33
  1.9 0.1 maximum_add_fusion.2
  2.0 0.1 fusion.33
  2.1 0.1 maximum_add_fusion.2
  2.3 0.1 fusion.33
  2.4 0.1 maximum_add_fusion.2
  2.5 0.1 fusion.33
  2.7 0.1 maximum_add_fusion.2
  2.8 0.1 fusion.33
  3.0 0.1 maximum_add_fusion.2
  3.1 0.1 fusion.33
  3.3 0.1 maximum_add_fusion.2
  3.4 0.1 fusion.33
  3.6 0.1 maximum_add_fusion.2
  3.7 0.1 fusion.33
  3.8 0.1 maximum_add_fusion.2
  4.0 0.1 fusion.33
  4.1 0.1 maximum_add_fusion.2
  4.3 0.1 fusion.33
  4.4 0.1 maximum_add_fusion.2
  4.5 4.8 %collective-permute-start = (f32[2,4096]{1,0:T(2,128)S(1)}, f32[2,4096]{1,0:T(2,128)S(1)}, u32[]{:S(2)}, u32[]{:S(2)}) collective-permute-start(f32[2,4096]{1,0:T(2,128)S(1)} %broadcast_multiply_fusion), channel_id=1, source_target_pairs={{0,8},{8,0},{16,24},{24,16},{32,40},{40,32},{48,56},{56,48},{64,72... | collective-permute-start | bytes 98312 | tf_op jit(solution)/shard_map/ppermute | solution.py:12
  9.4 1.8 %fusion.31 = (s32[1]{0:T(128)}, s32[1]{0:T(128)}, s32[1]{0:T(128)}, s32[1]{0:T(128)}, s32[1]{0:T(128)}, /*index=5*/s32[1]{0:T(128)}, s32[1]{0:T(128)}, s32[1]{0:...) fusion(s32[128]{0:T(128)} %param.10, s32[]{:T(128)S(6)} %select_n.148, s32[]{:T(128)S(6)} %select_n.166, ...), kind=kLoop, calls=%fused_computation.59 | loop fusion | bytes 144 | tf_op jit(solution)/shard_map/dynamic_slice | solution.py:57
  18.6 0.7 fusion.22
  19.3 0.7 fusion.24
  22.5 0.1 copy.11
  22.6 0.0 collective-permute-done
  22.6 0.2 multiply_reduce_fusion.2
  22.9 5.8 %collective-permute-start.1 = (f32[4,4096]{1,0:T(4,128)S(1)}, f32[4,4096]{1,0:T(4,128)S(1)}, u32[]{:S(2)}, u32[]{:S(2)}) collective-permute-start(f32[4,4096]{1,0:T(4,128)S(1)} %multiply_reduce_fusion.2), channel_id=1, source_target_pairs={{0,16},{8,24},{16,0},{24,8},{32,48},{40,56},{48,32},{56,40},{64,80... | collective-permute-start | bytes 196616 | tf_op jit(solution)/shard_map/ppermute | solution.py:12
  28.7 0.1 copy.10
  30.0 0.7 collective-permute-done.1
  30.8 0.4 multiply_reduce_fusion.1
  31.2 8.5 %collective-permute-start.2 = (f32[8,4096]{1,0:T(8,128)S(1)}, f32[8,4096]{1,0:T(8,128)S(1)}, u32[]{:S(2)}, u32[]{:S(2)}) collective-permute-start(f32[8,4096]{1,0:T(8,128)S(1)} %multiply_reduce_fusion.1), channel_id=1, source_target_pairs={{0,32},{8,40},{16,48},{24,56},{32,0},{40,8},{48,16},{56,24},{64,96... | collective-permute-start | bytes 393224 | tf_op jit(solution)/shard_map/ppermute | solution.py:12
  39.7 0.0 copy-done
  39.7 0.1 copy.9
  39.8 2.3 %collective-permute-done.2 = f32[8,4096]{1,0:T(8,128)S(1)} collective-permute-done((f32[8,4096]{1,0:T(8,128)S(1)}, f32[8,4096]{1,0:T(8,128)S(1)}, u32[]{:S(2)}, u32[]{:S(2)}) %collective-permute-start.2) | collective-permute-done | bytes 131104 | tf_op jit(solution)/shard_map/ppermute | solution.py:12
  42.2 0.8 multiply_reduce_fusion
  43.0 3.6 %collective-permute-start.3 = (f32[16,4096]{1,0:T(8,128)S(1)}, f32[16,4096]{1,0:T(8,128)S(1)}, u32[]{:S(2)}, u32[]{:S(2)}) collective-permute-start(f32[16,4096]{1,0:T(8,128)S(1)} %multiply_reduce_fusion), channel_id=1, source_target_pairs={{0,64},{8,72},{16,80},{24,88},{32,96},{40,104},{48,112},{56,120},{... | collective-permute-start | bytes 786440 | tf_op jit(solution)/shard_map/ppermute | solution.py:12
  50.1 0.2 collective-permute-done.3
  50.3 0.6 fusion.8
  50.9 4.4 %collective-permute-start.4 = (f32[32,4096]{1,0:T(8,128)S(1)}, f32[32,4096]{1,0:T(8,128)S(1)}, u32[]{:S(2)}, u32[]{:S(2)}) collective-permute-start(f32[32,4096]{1,0:T(8,128)S(1)} %fusion.8), channel_id=1, source_target_pairs={{0,128},{8,136},{16,144},{24,152},{32,160},{40,168},{48,176},{56,1... | collective-permute-start | bytes 1572872 | tf_op jit(solution)/shard_map/ppermute | solution.py:12
  59.5 18.3 %collective-permute-done.4 = f32[32,4096]{1,0:T(8,128)S(1)} collective-permute-done((f32[32,4096]{1,0:T(8,128)S(1)}, f32[32,4096]{1,0:T(8,128)S(1)}, u32[]{:S(2)}, u32[]{:S(2)}) %collective-permute-start.4) | collective-permute-done | bytes 524320 | tf_op jit(solution)/shard_map/ppermute | solution.py:12
  77.8 1.0 fusion.4
  78.8 8.4 %collective-permute-start.5 = (f32[64,4096]{1,0:T(8,128)S(1)}, f32[64,4096]{1,0:T(8,128)S(1)}, u32[]{:S(2)}, u32[]{:S(2)}) collective-permute-start(f32[64,4096]{1,0:T(8,128)S(1)} %fusion.4), channel_id=1, source_target_pairs={{0,256},{8,264},{16,272},{24,280},{32,288},{40,296},{48,304},{56,3... | collective-permute-start | bytes 3145736 | tf_op jit(solution)/shard_map/ppermute | solution.py:12
  90.9 42.1 %collective-permute-done.5 = f32[64,4096]{1,0:T(8,128)S(1)} collective-permute-done((f32[64,4096]{1,0:T(8,128)S(1)}, f32[64,4096]{1,0:T(8,128)S(1)}, u32[]{:S(2)}, u32[]{:S(2)}) %collective-permute-start.5) | collective-permute-done | bytes 1048608 | tf_op jit(solution)/shard_map/ppermute | solution.py:12
  133.0 0.0 copy-start.2
  133.0 0.0 copy-start.1
  133.0 1.9 %fusion = f32[128,4096]{1,0:T(8,128)S(1)} fusion(f32[64,4096]{1,0:T(8,128)S(1)} %collective-permute-done.5, f32[64,4096]{1,0:T(8,128)S(1)} %fusion.4, f32[128,64]{0,1:T(8,128)S(1)} %get-tuple-element.203, f32[128,64]{0,1:T(8,128)S(1)} %get-tuple-element.202), kind=kOutput, calls=%fused_computation.2 | convolution fusion | flops 805847040 | bytes 4259840 | tf_op jit(solution)/shard_map/dot_general | solution.py:72
  135.0 4.3 %collective-permute-start.6 = (f32[1,2,4096]{2,1,0:T(2,128)S(1)}, f32[1,2,4096]{2,1,0:T(2,128)S(1)}, u32[]{:S(2)}, u32[]{:S(2)}) collective-permute-start(f32[1,2,4096]{2,1,0:T(2,128)S(1)} %dynamic-slice_bitcast_fusion.2), channel_id=1, source_target_pairs={{0,1},{1,2},{2,3},{3,4},{4,5},{5,6},{6,7},{8,9},{9,10},{10,11},{11... | collective-permute-start | bytes 98312 | tf_op jit(solution)/shard_map/ppermute | solution.py:23
  139.3 1.9 %collective-permute-start.7 = (f32[1,2,4096]{2,1,0:T(2,128)S(1)}, f32[1,2,4096]{2,1,0:T(2,128)S(1)}, u32[]{:S(2)}, u32[]{:S(2)}) collective-permute-start(f32[1,2,4096]{2,1,0:T(2,128)S(1)} %dynamic-slice_bitcast_fusion.2), channel_id=1, source_target_pairs={{1,0},{2,1},{3,2},{4,3},{5,4},{6,5},{7,6},{9,8},{10,9},{11,10},{12... | collective-permute-start | bytes 98312 | tf_op jit(solution)/shard_map/ppermute | solution.py:25
  141.3 0.0 copy-done.2
  141.3 0.6 fusion.30
  141.9 0.0 collective-permute-done.6
  141.9 2.7 %collective-permute-done.7 = f32[1,2,4096]{2,1,0:T(2,128)S(1)} collective-permute-done((f32[1,2,4096]{2,1,0:T(2,128)S(1)}, f32[1,2,4096]{2,1,0:T(2,128)S(1)}, u32[]{:S(2)}, u32[]{:S(2)}) %collective-permute-start.7) | collective-permute-done | bytes 32800 | tf_op jit(solution)/shard_map/ppermute | solution.py:25
  144.6 0.0 copy-done.1
  144.6 2.5 %fusion.18 = f32[1,2,4096]{2,1,0:T(2,128)} fusion(f32[1,2,4096]{2,1,0:T(2,128)S(1)} %collective-permute-done.7, f32[1,2,4096]{2,1,0:T(2,128)S(1)} %collective-permute-done.6, f32[128,4096]{1,0:T(8,128)S(1)} %fusion, s32[]{:T(128)S(6)} %select_n.172, bf16[1,2,4096]{2,1,0:T(2,128)(2,1)S(1)} %copy-done.1, f32[]{:T(128)} %bitcast.30, f32[]{:T(128)} %bitcast.29, ...), kind=kLoop, calls=%fused_computation.27 | loop fusion | flops 57344 | bytes 147472 | tf_op jit(solution)/shard_map/broadcast_in_dim | solution.py:90
  (13 shorter events, 0.2 us)
Async XLA Ops:
  0.0 39.7 %copy-start = (f32[4,128,64]{1,2,0:T(8,128)S(1)}, f32[4,128,64]{1,2,0:T(8,128)}, u32[]{:S(2)}) copy-start(f32[4,128,64]{1,2,0:T(8,128)} %param.9) | copy-start | bytes 393220
  4.5 18.1 %collective-permute-start = (f32[2,4096]{1,0:T(2,128)S(1)}, f32[2,4096]{1,0:T(2,128)S(1)}, u32[]{:S(2)}, u32[]{:S(2)}) collective-permute-start(f32[2,4096]{1,0:T(2,128)S(1)} %broadcast_multiply_fusion), channel_id=1, source_target_pairs={{0,8},{8,0},{16,24},{24,16},{32,40},{40,32},{48,56},{56,48},{64,72... | collective-permute-start | bytes 98312 | tf_op jit(solution)/shard_map/ppermute | solution.py:12
  22.9 7.9 %collective-permute-start.1 = (f32[4,4096]{1,0:T(4,128)S(1)}, f32[4,4096]{1,0:T(4,128)S(1)}, u32[]{:S(2)}, u32[]{:S(2)}) collective-permute-start(f32[4,4096]{1,0:T(4,128)S(1)} %multiply_reduce_fusion.2), channel_id=1, source_target_pairs={{0,16},{8,24},{16,0},{24,8},{32,48},{40,56},{48,32},{56,40},{64,80... | collective-permute-start | bytes 196616 | tf_op jit(solution)/shard_map/ppermute | solution.py:12
  31.2 11.0 %collective-permute-start.2 = (f32[8,4096]{1,0:T(8,128)S(1)}, f32[8,4096]{1,0:T(8,128)S(1)}, u32[]{:S(2)}, u32[]{:S(2)}) collective-permute-start(f32[8,4096]{1,0:T(8,128)S(1)} %multiply_reduce_fusion.1), channel_id=1, source_target_pairs={{0,32},{8,40},{16,48},{24,56},{32,0},{40,8},{48,16},{56,24},{64,96... | collective-permute-start | bytes 393224 | tf_op jit(solution)/shard_map/ppermute | solution.py:12
  43.0 7.3 %collective-permute-start.3 = (f32[16,4096]{1,0:T(8,128)S(1)}, f32[16,4096]{1,0:T(8,128)S(1)}, u32[]{:S(2)}, u32[]{:S(2)}) collective-permute-start(f32[16,4096]{1,0:T(8,128)S(1)} %multiply_reduce_fusion), channel_id=1, source_target_pairs={{0,64},{8,72},{16,80},{24,88},{32,96},{40,104},{48,112},{56,120},{... | collective-permute-start | bytes 786440 | tf_op jit(solution)/shard_map/ppermute | solution.py:12
  50.9 26.9 %collective-permute-start.4 = (f32[32,4096]{1,0:T(8,128)S(1)}, f32[32,4096]{1,0:T(8,128)S(1)}, u32[]{:S(2)}, u32[]{:S(2)}) collective-permute-start(f32[32,4096]{1,0:T(8,128)S(1)} %fusion.8), channel_id=1, source_target_pairs={{0,128},{8,136},{16,144},{24,152},{32,160},{40,168},{48,176},{56,1... | collective-permute-start | bytes 1572872 | tf_op jit(solution)/shard_map/ppermute | solution.py:12
  78.8 54.1 %collective-permute-start.5 = (f32[64,4096]{1,0:T(8,128)S(1)}, f32[64,4096]{1,0:T(8,128)S(1)}, u32[]{:S(2)}, u32[]{:S(2)}) collective-permute-start(f32[64,4096]{1,0:T(8,128)S(1)} %fusion.4), channel_id=1, source_target_pairs={{0,256},{8,264},{16,272},{24,280},{32,288},{40,296},{48,304},{56,3... | collective-permute-start | bytes 3145736 | tf_op jit(solution)/shard_map/ppermute | solution.py:12
  133.0 8.3 %copy-start.2 = (f32[3]{0:T(128)S(1)}, f32[3]{0:T(128)}, u32[]{:S(2)}) copy-start(f32[3]{0:T(128)} %param.11) | copy-start | bytes 40
  133.0 11.6 %copy-start.1 = (bf16[1,2,4096]{2,1,0:T(2,128)(2,1)S(1)}, bf16[1,2,4096]{2,1,0:T(2,128)(2,1)}, u32[]{:S(2)}) copy-start(bf16[1,2,4096]{2,1,0:T(2,128)(2,1)} %param.8) | copy-start | bytes 49156
  135.0 6.9 %collective-permute-start.6 = (f32[1,2,4096]{2,1,0:T(2,128)S(1)}, f32[1,2,4096]{2,1,0:T(2,128)S(1)}, u32[]{:S(2)}, u32[]{:S(2)}) collective-permute-start(f32[1,2,4096]{2,1,0:T(2,128)S(1)} %dynamic-slice_bitcast_fusion.2), channel_id=1, source_target_pairs={{0,1},{1,2},{2,3},{3,4},{4,5},{5,6},{6,7},{8,9},{9,10},{10,11},{11... | collective-permute-start | bytes 98312 | tf_op jit(solution)/shard_map/ppermute | solution.py:23
  139.3 5.2 %collective-permute-start.7 = (f32[1,2,4096]{2,1,0:T(2,128)S(1)}, f32[1,2,4096]{2,1,0:T(2,128)S(1)}, u32[]{:S(2)}, u32[]{:S(2)}) collective-permute-start(f32[1,2,4096]{2,1,0:T(2,128)S(1)} %dynamic-slice_bitcast_fusion.2), channel_id=1, source_target_pairs={{1,0},{2,1},{3,2},{4,3},{5,4},{6,5},{7,6},{9,8},{10,9},{11,10},{12... | collective-permute-start | bytes 98312 | tf_op jit(solution)/shard_map/ppermute | solution.py:25
where the time goes:
time: 149 us; the launch traced here: 147 us
  waiting for transfers between devices  66.3 us (44%)
  starting transfers between devices  41.8 us (28%)
  between operations  22.7 us (15%)
  local copies, waits for them, and re-layouts  5.89 us (4%)
  other arithmetic  5.82 us (4%)
  matrix products  3.59 us (2%)
    ppermute x6, waiting for transfers between devices, partner_2(): return lax.ppermute(value, axis, pairs)  63.6 us
    ppermute x6, starting transfers between devices, partner_2(): return lax.ppermute(value, axis, pairs)  35.5 us
    ppermute x1, starting transfers between devices, padded_2(): lax.ppermute(tail, axis, [(i, (i + 1) % count) for i in range(ends)])  4.35 us
    dot_general x3, matrix products, refine(): return jnp.dot(joined, stacked, precision=lax.Precision.HIGHEST)  3.59 us
  transfers between devices with their start and end apart: 8, of which 6 were waited for; matrix products, arithmetic and copies ran while one was open for 3% of the time, Pallas kernels for 0%

commit v1 on v0

v1 whole, which is shorter than its diff:
```python
import functools
import math

import jax
import jax.numpy as jnp
from jax import lax
from jax.experimental import pallas as pl
from jax.experimental.pallas import tpu as pltpu
from jax.sharding import PartitionSpec as P

MESH = pl.DeviceIdType.MESH
SIDE = 8
LANES = 128
OWNERS = ((0, 0), (1, 0), (2, 0), (3, 0), (4, 0), (5, 0), (6, 0), (7, 0))
BLOCKS = len(OWNERS)


def parts_of(value):
    high = value.astype(jnp.bfloat16)
    low = (value - high.astype(jnp.float32)).astype(jnp.bfloat16)
    return high, low


def tree_matrix(bank_ref, index_ref, levels, size):
    iota = lambda shape, dim: lax.broadcasted_iota(jnp.int32, shape, dim)
    kinds, half = bank_ref.shape[:2]
    index = jnp.broadcast_to(index_ref[...].astype(jnp.float32), (8, size))
    product = None
    for level in range(1, levels + 1):
        width = size >> level
        row, col = iota((size, size), 0), iota((size, size), 1)
        chosen = (row == (1 << level) + col // width).astype(jnp.float32)
        kind = jnp.dot(index, chosen, preferred_element_type=jnp.float32)[0:1]
        block = jnp.zeros((2 * width, size), jnp.float32)
        pick = iota((half, size), 0) == iota((half, size), 1) % width
        for k in range(kinds):
            place = jnp.where(pick & (jnp.abs(kind - k) < 0.5), 1.0, 0.0)
            block += lax.dot_general(
                bank_ref[k, :, :],
                place,
                (((0,), (0,)), ((), ())),
                precision=lax.Precision.HIGHEST,
                preferred_element_type=jnp.float32,
            )[: 2 * width]
        if 2 * width < 8:
            block = jnp.concatenate([block] * (8 // (2 * width)), axis=0)
        factor = jnp.concatenate([block] * (size // block.shape[0]), axis=0)
        factor = jnp.where(row // (2 * width) == col // (2 * width), factor, 0.0)
        if product is None:
            product = factor
        else:
            product = jnp.dot(
                product, factor, precision=lax.Precision.HIGHEST, preferred_element_type=jnp.float32
            )
    return product


def kernel(
    sino_any, bank_any, index_any, taps_any, out_ref,
    sino_ref, bank_ref, index_ref, taps_ref, send_buf, leaf_buf, result_buf, image_buf, tree_buf,
    local_sem, leaf_send, leaf_recv, image_send, image_recv,
):
    views, columns = sino_ref.shape
    groups = SIDE * SIDE
    chunks = columns // LANES
    per_block = chunks // BLOCKS
    slices = lax.axis_size("cuts")
    group = lax.axis_index("angle")
    cut = lax.axis_index("cuts")

    mine = [group == y * SIDE + z for y, z in OWNERS]
    is_owner = functools.reduce(jnp.logical_or, mine)
    block_id = sum(jnp.where(hit, b, 0) for b, hit in enumerate(mine))
    owner_int = is_owner.astype(jnp.int32)
    has_side = [cut > 0, True, cut < slices - 1]

    def rows(index):
        return pl.ds(2 * index, 2)

    barrier = pltpu.get_barrier_semaphore()
    sino_copy = pltpu.make_async_copy(sino_any, sino_ref, local_sem.at[0])
    sino_copy.start()

    @pl.when(is_owner)
    def _():
        bank_copy = pltpu.make_async_copy(bank_any, bank_ref, local_sem.at[1])
        index_copy = pltpu.make_async_copy(index_any, index_ref, local_sem.at[2])
        taps_copy = pltpu.make_async_copy(taps_any, taps_ref, local_sem.at[3])
        bank_copy.start()
        index_copy.start()
        taps_copy.start()

        def announce(step, carry):
            for side in range(3):
                target = lax.rem(cut + side - 1 + slices, slices)
                valid = step != group if side == 1 else has_side[side]

                @pl.when(valid)
                def _():
                    pl.semaphore_signal(barrier, inc=1, device_id=(step, target), device_id_type=MESH)

            return carry

        lax.fori_loop(0, groups, announce, 0)
        bank_copy.wait()
        index_copy.wait()
        taps_copy.wait()

    sino_copy.wait()
    total = jnp.sum(sino_ref[...].astype(jnp.float32), axis=0, keepdims=True)
    sub = lax.broadcasted_iota(jnp.int32, (8, LANES), 0)
    tiles = []
    for t in range(chunks // 8):
        tile = jnp.zeros((8, LANES), jnp.float32)
        for i in range(8):
            c = t * 8 + i
            piece = jnp.broadcast_to(total[:, c * LANES : (c + 1) * LANES], (8, LANES))
            tile = jnp.where(sub == i, piece, tile)
        tiles.append(tile)
    summed = jnp.concatenate(tiles, axis=0)
    lane = lax.broadcasted_iota(jnp.int32, (chunks, LANES), 1)
    chunk = lax.broadcasted_iota(jnp.int32, (chunks, LANES), 0)
    shift = lax.div(group, 2) - groups // 4
    for r, amount in enumerate((-1 - shift, shift)):
        turned = pltpu.roll(summed, lax.rem(amount + LANES, LANES), 1)
        before = jnp.where(chunk == 0, 0.0, pltpu.roll(turned, 1, 0))
        after = jnp.where(chunk == chunks - 1, 0.0, pltpu.roll(turned, chunks - 1, 0))
        source = lane - amount
        leaf = jnp.where(source < 0, before, jnp.where(source >= LANES, after, turned))
        for b in range(BLOCKS):
            send_buf[2 * b + r, :, :] = leaf[b * per_block : (b + 1) * per_block, :]

    n_sides = 1 + (cut > 0).astype(jnp.int32) + (cut < slices - 1).astype(jnp.int32)
    pl.semaphore_wait(barrier, n_sides * BLOCKS - owner_int)

    def leaf_copy(b, side):
        y, z = OWNERS[b]
        return pltpu.make_async_remote_copy(
            src_ref=send_buf.at[rows(b)],
            dst_ref=leaf_buf.at[2 - side, rows(group)],
            send_sem=leaf_send,
            recv_sem=leaf_recv.at[2 - side],
            device_id=(y * SIDE + z, lax.rem(cut + side - 1 + slices, slices)),
            device_id_type=MESH,
        )

    for b in range(BLOCKS):
        for side in range(3):
            if side == 1:
                valid = jnp.logical_not(mine[b])
            else:
                valid = has_side[side]

            @pl.when(valid)
            def _():
                leaf_copy(b, side).start()

    @pl.when(is_owner)
    def _():
        leaf_buf[1, rows(group)] = send_buf[rows(block_id)]
        tree = tree_matrix(bank_ref, index_ref, 6, 2 * groups) * (1.0 / math.sqrt(views))
        high, low = parts_of(tree)
        tree_buf[...] = jnp.concatenate([high, low, high], axis=1)
        for side in range(3):
            count = groups - 1 if side == 1 else groups

            @pl.when(has_side[side])
            def _():
                done = leaf_buf.at[side, pl.ds(0, 2 * count)]
                pltpu.make_async_copy(done, done, leaf_recv.at[side]).wait()

        mixed = []
        for i in range(per_block):
            term = None
            for side in range(3):
                value = taps_ref[side] * leaf_buf[side, :, i, :]
                if side != 1:
                    value = jnp.where(has_side[side], value, 0.0)
                term = value if term is None else term + value
            mixed.append(term)
        high, low = parts_of(jnp.concatenate(mixed, axis=1))
        image = jnp.dot(
            tree_buf[...], jnp.concatenate([high, high, low], axis=0), preferred_element_type=jnp.float32
        )
        for i in range(per_block):
            result_buf[:, i, :] = image[:, i * LANES : (i + 1) * LANES]

        image_buf[rows(block_id)] = result_buf[rows(group)]

        def give(step, carry):
            @pl.when(step != group)
            def _():
                pltpu.make_async_remote_copy(
                    src_ref=result_buf.at[rows(step)],
                    dst_ref=image_buf.at[rows(block_id)],
                    send_sem=image_send,
                    recv_sem=image_recv,
                    device_id=(step, cut),
                    device_id_type=MESH,
                ).start()

            return carry

        lax.fori_loop(0, groups, give, 0)
        got = image_buf.at[pl.ds(0, 2 * (BLOCKS - 1))]
        pltpu.make_async_copy(got, got, image_recv).wait()

    @pl.when(jnp.logical_not(is_owner))
    def _():
        pltpu.make_async_copy(image_buf, image_buf, image_recv).wait()

    for b in range(BLOCKS):
        for i in range(per_block):
            c = b * per_block + i
            out_ref[:, c * LANES : (c + 1) * LANES] = image_buf[2 * b : 2 * b + 2, i, :]

    for b in range(BLOCKS):
        for side in range(3):
            if side == 1:
                valid = jnp.logical_not(mine[b])
            else:
                valid = has_side[side]

            @pl.when(valid)
            def _():
                leaf_copy(b, side).wait_send()

    @pl.when(is_owner)
    def _():
        sent = result_buf.at[pl.ds(0, 2 * (groups - 1))]
        pltpu.make_async_copy(sent, sent, image_send).wait()


def shards(sinogram, estimate, interp_bank, interp_index, slice_taps):
    _, views, columns = sinogram.shape
    groups = SIDE * SIDE
    chunks = columns // LANES
    per_block = chunks // BLOCKS
    size = 2 * groups
    bank = jnp.swapaxes(interp_bank, 1, 2)
    operands = (sinogram[0], bank, interp_index.reshape(1, -1), slice_taps)
    held = [pltpu.with_memory_space_constraint(x, pltpu.HBM) for x in operands]
    mixed = pl.pallas_call(
        kernel,
        out_shape=pltpu.VMEM((2, columns), jnp.float32),
        in_specs=[
            pl.BlockSpec(memory_space=pltpu.HBM),
            pl.BlockSpec(memory_space=pltpu.HBM),
            pl.BlockSpec(memory_space=pltpu.HBM),
            pl.BlockSpec(memory_space=pltpu.HBM),
        ],
        out_specs=pl.BlockSpec(memory_space=pltpu.VMEM),
        scratch_shapes=[
            pltpu.VMEM((views, columns), jnp.bfloat16),
            pltpu.VMEM(bank.shape, jnp.float32),
            pltpu.VMEM((1, size), jnp.int32),
            pltpu.SMEM((3,), jnp.float32),
            pltpu.VMEM((2 * BLOCKS, per_block, LANES), jnp.float32),
            pltpu.VMEM((3, size, per_block, LANES), jnp.float32),
            pltpu.VMEM((size, per_block, LANES), jnp.float32),
            pltpu.VMEM((2 * BLOCKS, per_block, LANES), jnp.float32),
            pltpu.VMEM((size, 3 * size), jnp.bfloat16),
            pltpu.SemaphoreType.DMA((4,)),
            pltpu.SemaphoreType.DMA,
            pltpu.SemaphoreType.DMA((3,)),
            pltpu.SemaphoreType.DMA,
            pltpu.SemaphoreType.DMA,
        ],
        compiler_params=pltpu.CompilerParams(
            collective_id=0, has_side_effects=True, vmem_limit_bytes=32 * 1024 * 1024
        ),
    )(*held)
    return (estimate[0].astype(jnp.float32) - mixed)[None]


def solution(mesh):
    in_specs = (P("cuts", "angle", None), P("cuts", "angle", None), P(), P(), P())
    out_specs = P("cuts", "angle", None)
    return jax.shard_map(shards, mesh=mesh, in_specs=in_specs, out_specs=out_specs, check_vma=False)
```

time: 149 us -> 31.7 us (0.21)
  the two profiles are of different devices: /device:TPU:1 before, /device:TPU:18 now
where the time goes in v1:
time: 31.7 us; the launch traced here: 31.6 us
  Pallas kernels  30.9 us (97%)
  other arithmetic  0.63 us (2%)
    pallas_call x1, Pallas kernels, shards(): pl.pallas_call(kernel, out_shape=pltpu.VMEM((2, columns), jnp.float32), i...  30.9 us
    broadcast_in_dim x1, other arithmetic, shards(): return (estimate[0].astype(jnp.float32) - mixed)[None]  0.63 us

profile of v1, /device:TPU:18, one launch (start us, length us, event | category | flops | bytes accessed | tf_op | source)
XLA Modules:
  0.0 31.6 jit_solution(3736564787366780467)
XLA Ops:
  0.0 0.0 copy-start
  0.0 30.9 %shard_map.55 = f32[2,4096]{1,0:T(2,128)S(1)} custom-call(bf16[12,4096]{1,0:T(8,128)(2,1)} %bitcast.8, f32[4,64,128]{2,1,0:T(8,128)} %bitcast.9, s32[1,128]{1,0:T(1,128)} %bitcast.10, f32[3]{0:T(128)} %taps_any.1), custom_call_target="tpu_custom_call" | custom-call | tf_op jit(solution)/shard_map/pallas_call | solution.py:243
  30.9 0.0 copy-done
  31.0 0.6 %fusion = f32[1,2,4096]{2,1,0:T(2,128)} fusion(f32[2,4096]{1,0:T(2,128)S(1)} %shard_map.55, bf16[1,2,4096]{2,1,0:T(2,128)(2,1)S(1)} %copy-done), kind=kLoop, calls=%fused_computation.1 | loop fusion | flops 16384 | bytes 81920 | tf_op jit(solution)/shard_map/broadcast_in_dim | solution.py:273
Async XLA Ops:
  0.0 31.0 %copy-start = (bf16[1,2,4096]{2,1,0:T(2,128)(2,1)S(1)}, bf16[1,2,4096]{2,1,0:T(2,128)(2,1)}, u32[]{:S(2)}) copy-start(bf16[1,2,4096]{2,1,0:T(2,128)(2,1)} %param.6) | copy-start | bytes 49156

commit v2 on v1

v2 whole, which is shorter than its diff:
```python
import functools
import math

import jax
import jax.numpy as jnp
from jax import lax
from jax.experimental import pallas as pl
from jax.experimental.pallas import tpu as pltpu
from jax.sharding import PartitionSpec as P

MESH = pl.DeviceIdType.MESH
SIDE = 8
CORES = 2
LANES = 128
GROUPS = SIDE * SIDE
SIZE = 2 * GROUPS
OWNERS = ((0, 1), (1, 0), (2, 0), (3, 0), (4, 0), (5, 0), (6, 0), (7, 0))
BLOCKS = len(OWNERS) * CORES


def parts_of(value):
    high = value.astype(jnp.bfloat16)
    low = (value - high.astype(jnp.float32)).astype(jnp.bfloat16)
    return high, low


def iota(shape, dim):
    return lax.broadcasted_iota(jnp.int32, shape, dim)


def tree_matrix(bank_ref, index_ref):
    kinds, half = bank_ref.shape[:2]
    levels = GROUPS.bit_length() - 1
    index = jnp.broadcast_to(index_ref[...].astype(jnp.float32), (8, SIZE))
    product = None
    for level in range(1, levels + 1):
        width = SIZE >> level
        row, col = iota((SIZE, SIZE), 0), iota((SIZE, SIZE), 1)
        chosen = (row == (1 << level) + col // width).astype(jnp.float32)
        kind = jnp.dot(index, chosen, preferred_element_type=jnp.float32)[0:1]
        block = jnp.zeros((2 * width, SIZE), jnp.float32)
        pick = iota((half, SIZE), 0) == iota((half, SIZE), 1) % width
        for k in range(kinds):
            place = jnp.where(pick & (jnp.abs(kind - k) < 0.5), 1.0, 0.0)
            block += lax.dot_general(
                bank_ref[k, :, :],
                place,
                (((0,), (0,)), ((), ())),
                precision=lax.Precision.HIGHEST,
                preferred_element_type=jnp.float32,
            )[: 2 * width]
        if 2 * width < 8:
            block = jnp.concatenate([block] * (8 // (2 * width)), axis=0)
        factor = jnp.concatenate([block] * (SIZE // block.shape[0]), axis=0)
        factor = jnp.where(row // (2 * width) == col // (2 * width), factor, 0.0)
        if product is None:
            product = factor
        else:
            product = jnp.dot(
                product, factor, precision=lax.Precision.HIGHEST, preferred_element_type=jnp.float32
            )
    return product


def far_first(turn):
    back = lax.rem(turn, 2)
    return SIDE // 2 + (1 - 2 * back) * lax.div(turn + back, 2)


def slot_of(group):
    return lax.rem(group, 2) * (GROUPS // 2) + lax.div(group, 2)


def kernel(
    sino_any, bank_any, index_any, taps_any, out_ref,
    sino_ref, bank_ref, index_ref, taps_ref, send_buf, leaf_buf, result_buf, image_buf, tree_buf,
    local_sem, leaf_send, leaf_recv, image_send, image_recv,
):
    views, columns = sino_ref.shape
    per_block = columns // LANES // BLOCKS
    window = per_block + 1
    slices = lax.axis_size("cuts")
    group = lax.axis_index("angle")
    cut = lax.axis_index("cuts")
    core = lax.rem(cut, CORES)
    first = cut - core
    here = [group == y * SIDE + z for y, z in OWNERS]
    is_owner = functools.reduce(jnp.logical_or, here)
    mine = core + sum(jnp.where(hit, CORES * i, 0) for i, hit in enumerate(here))
    half = GROUPS // 2

    has_side = [first > 0, True, True, first + CORES < slices]
    side_cut = [lax.rem(first + side - 1 + slices, slices) for side in range(4)]

    barrier = pltpu.get_barrier_semaphore()
    sino_copy = pltpu.make_async_copy(sino_any, sino_ref, local_sem.at[0])
    sino_copy.start()

    @pl.when(is_owner)
    def _():
        bank_copy = pltpu.make_async_copy(bank_any, bank_ref, local_sem.at[1])
        index_copy = pltpu.make_async_copy(index_any, index_ref, local_sem.at[2])
        taps_copy = pltpu.make_async_copy(taps_any, taps_ref, local_sem.at[3])
        bank_copy.start()
        index_copy.start()
        taps_copy.start()

        def announce(step, carry):
            y = lax.rem(lax.div(group, SIDE) + far_first(lax.rem(step, SIDE)), SIDE)
            z = lax.rem(group + far_first(lax.div(step, SIDE)), SIDE)
            target = y * SIDE + z
            for side in range(4):
                valid = has_side[side]
                if side in (1, 2):
                    valid = jnp.logical_or(target != group, core != side - 1)

                @pl.when(valid)
                def _():
                    pl.semaphore_signal(barrier, inc=1, device_id=(target, side_cut[side]), device_id_type=MESH)

            return carry

        lax.fori_loop(0, GROUPS, announce, 0)
        bank_copy.wait()
        index_copy.wait()
        taps_copy.wait()

    sino_copy.wait()
    total = jnp.sum(sino_ref[...].astype(jnp.float32), axis=0, keepdims=True)
    margin = jnp.zeros((1, LANES // 2), jnp.float32)
    total = jnp.concatenate([margin, total, margin], axis=1)
    for b in range(BLOCKS):
        for c in range(window):
            start = (b * per_block + c) * LANES
            send_buf[b, c : c + 1, :] = total[:, start : start + LANES]

    other = jnp.where(core == 0, cut - 1, cut + 1)
    has_other = jnp.where(core == 0, cut > 0, cut < slices - 1)
    other_first = lax.rem(jnp.where(core == 0, cut - CORES, cut + 1) + slices, slices)
    other_side = jnp.where(core == 0, 3, 0)
    n_owners = BLOCKS + jnp.where(has_other, BLOCKS, 0) - jnp.where(is_owner, 1, 0)
    pl.semaphore_wait(barrier, n_owners)

    def leaf_copy(b, plane):
        base, side = (first, 1 + core) if plane == 0 else (other_first, other_side)
        return pltpu.make_async_remote_copy(
            src_ref=send_buf.at[b],
            dst_ref=leaf_buf.at[side, slot_of(group)],
            send_sem=leaf_send,
            recv_sem=leaf_recv.at[side],
            device_id=(OWNERS[b // CORES][0] * SIDE + OWNERS[b // CORES][1], base + b % CORES),
            device_id_type=MESH,
        )

    def each_leaf(act):
        for plane in range(2):
            for b in range(BLOCKS):
                valid = has_other
                if plane == 0:
                    valid = jnp.logical_not(jnp.logical_and(is_owner, mine == b))

                @pl.when(valid)
                def _():
                    act(leaf_copy(b, plane))

    each_leaf(lambda copy: copy.start())

    @pl.when(is_owner)
    def _():
        leaf_buf[1 + core, slot_of(group)] = send_buf[mine]
        row, col = iota((SIZE, SIZE), 0), iota((SIZE, SIZE), 1)
        natural = 4 * (col % half) + 2 * (col % GROUPS // half) + col // GROUPS
        order = (row == natural).astype(jnp.bfloat16)
        tree = tree_matrix(bank_ref, index_ref) * (1.0 / math.sqrt(views))
        high, low = [
            jnp.dot(part, order, preferred_element_type=jnp.float32).astype(jnp.bfloat16) for part in parts_of(tree)
        ]
        tree_buf[...] = jnp.concatenate([high, low, high], axis=1)

        for side in range(4):
            def wait(count):
                done = leaf_buf.at[side, pl.ds(0, count)]
                pltpu.make_async_copy(done, done, leaf_recv.at[side]).wait()

            if side in (1, 2):
                own = core == side - 1
                pl.when(own)(lambda: wait(GROUPS - 1))
                pl.when(jnp.logical_not(own))(lambda: wait(GROUPS))
            else:
                pl.when(has_side[side])(lambda: wait(GROUPS))

        lane, place = iota((half, LANES), 1), iota((half, LANES), 0)
        moved = [half // 2 - 1 - place, place - half // 2]
        back = lax.rem(lane - moved[0] + LANES // 2 + LANES, LANES)
        leaves = []
        for e in range(CORES):
            mixed = [[None] * 2 for _ in range(window)]
            for c in range(window):
                term = None
                for tap in range(3):
                    value = taps_ref[tap] * leaf_buf[e + tap, :, c, :]
                    if e + tap in (0, 3):
                        value = jnp.where(has_side[e + tap], value, 0.0)
                    term = value if term is None else term + value
                mixed[c] = [term[:half], term[half:]]
            rows = []
            for r in range(2):
                for h in range(2):
                    turned = []
                    for c in range(window):
                        if r == 1:
                            turned.append(
                                pltpu.roll(mixed[c][h], LANES // 2 - half // 2, 1, stride=1, stride_axis=0)
                            )
                        else:
                            turned.append(jnp.take_along_axis(mixed[c][h], back, axis=1))
                    rows.append(
                        jnp.concatenate(
                            [
                                jnp.where(lane - moved[r] < LANES // 2, turned[i], turned[i + 1])
                                for i in range(per_block)
                            ],
                            axis=1,
                        )
                    )
            leaves.append(jnp.concatenate(rows, axis=0))
        high, low = parts_of(jnp.concatenate(leaves, axis=1))
        image = jnp.dot(
            tree_buf[...], jnp.concatenate([high, high, low], axis=0), preferred_element_type=jnp.float32
        )
        for e in range(CORES):
            for i in range(per_block):
                start = (e * per_block + i) * LANES
                result_buf[e, :, i, :] = image[:, start : start + LANES]

        image_buf[pl.ds(2 * mine, 2)] = result_buf[core, pl.ds(2 * group, 2)]

        def give(step, carry):
            turn = lax.rem(step, SIDE)
            y = jnp.where(turn < SIDE // 2, turn, SIDE + SIDE // 2 - 1 - turn)
            target = y * SIDE + lax.div(step, SIDE)
            for e in range(CORES):

                @pl.when(jnp.logical_or(target != group, core != e))
                def _():
                    pltpu.make_async_remote_copy(
                        src_ref=result_buf.at[e, pl.ds(2 * target, 2)],
                        dst_ref=image_buf.at[pl.ds(2 * mine, 2)],
                        send_sem=image_send,
                        recv_sem=image_recv,
                        device_id=(target, first + e),
                        device_id_type=MESH,
                    ).start()

            return carry

        lax.fori_loop(0, GROUPS, give, 0)
        got = image_buf.at[pl.ds(0, 2 * (BLOCKS - 1))]
        pltpu.make_async_copy(got, got, image_recv).wait()

    @pl.when(jnp.logical_not(is_owner))
    def _():
        pltpu.make_async_copy(image_buf, image_buf, image_recv).wait()

    for b in range(BLOCKS):
        for i in range(per_block):
            c = b * per_block + i
            out_ref[:, c * LANES : (c + 1) * LANES] = image_buf[2 * b : 2 * b + 2, i, :]

    each_leaf(lambda copy: copy.wait_send())

    @pl.when(is_owner)
    def _():
        for e in range(CORES):
            own = core == e

            def wait(count):
                sent = result_buf.at[e, pl.ds(0, 2 * count)]
                pltpu.make_async_copy(sent, sent, image_send).wait()

            pl.when(own)(lambda: wait(GROUPS - 1))
            pl.when(jnp.logical_not(own))(lambda: wait(GROUPS))


def shards(sinogram, estimate, interp_bank, interp_index, slice_taps):
    _, views, columns = sinogram.shape
    per_block = columns // LANES // BLOCKS
    bank = jnp.swapaxes(interp_bank, 1, 2)
    operands = (sinogram[0], bank, interp_index.reshape(1, -1), slice_taps)
    held = [pltpu.with_memory_space_constraint(x, pltpu.HBM) for x in operands]
    mixed = pl.pallas_call(
        kernel,
        out_shape=pltpu.VMEM((2, columns), jnp.float32),
        in_specs=[pl.BlockSpec(memory_space=pltpu.HBM)] * 4,
        out_specs=pl.BlockSpec(memory_space=pltpu.VMEM),
        scratch_shapes=[
            pltpu.VMEM((views, columns), jnp.bfloat16),
            pltpu.VMEM(bank.shape, jnp.float32),
            pltpu.VMEM((1, SIZE), jnp.int32),
            pltpu.SMEM((3,), jnp.float32),
            pltpu.VMEM((BLOCKS, per_block + 1, LANES), jnp.float32),
            pltpu.VMEM((4, GROUPS, per_block + 1, LANES), jnp.float32),
            pltpu.VMEM((CORES, SIZE, per_block, LANES), jnp.float32),
            pltpu.VMEM((2 * BLOCKS, per_block, LANES), jnp.float32),
            pltpu.VMEM((SIZE, 3 * SIZE), jnp.bfloat16),
            pltpu.SemaphoreType.DMA((4,)),
            pltpu.SemaphoreType.DMA,
            pltpu.SemaphoreType.DMA((4,)),
            pltpu.SemaphoreType.DMA,
            pltpu.SemaphoreType.DMA,
        ],
        compiler_params=pltpu.CompilerParams(
            collective_id=0, has_side_effects=True, vmem_limit_bytes=32 * 1024 * 1024
        ),
    )(*held)
    return (estimate[0].astype(jnp.float32) - mixed)[None]


def solution(mesh):
    in_specs = (P("cuts", "angle", None), P("cuts", "angle", None), P(), P(), P())
    out_specs = P("cuts", "angle", None)
    return jax.shard_map(shards, mesh=mesh, in_specs=in_specs, out_specs=out_specs, check_vma=False)
```

time: 31.7 us -> 27 us (0.85)
  the two profiles are of different devices: /device:TPU:18 before, /device:TPU:1 now
where the time goes in v2:
time: 27 us; the launch traced here: 26.8 us
  Pallas kernels  26.1 us (97%)
  other arithmetic  0.63 us (2%)
    pallas_call x1, Pallas kernels, shards(): pl.pallas_call(kernel, out_shape=pltpu.VMEM((2, columns), jnp.float32), i...  26.1 us
    broadcast_in_dim x1, other arithmetic, shards(): return (estimate[0].astype(jnp.float32) - mixed)[None]  0.63 us

profile of v2, /device:TPU:1, one launch (start us, length us, event | category | flops | bytes accessed | tf_op | source)
XLA Modules:
  0.0 26.8 jit_solution(5372591421584004601)
XLA Ops:
  0.0 0.0 copy-start
  0.0 26.1 %shard_map.55 = f32[2,4096]{1,0:T(2,128)S(1)} custom-call(bf16[12,4096]{1,0:T(8,128)(2,1)} %bitcast.8, f32[4,64,128]{2,1,0:T(8,128)} %bitcast.9, s32[1,128]{1,0:T(1,128)} %bitcast.10, f32[3]{0:T(128)} %taps_any.1), custom_call_target="tpu_custom_call" | custom-call | tf_op jit(solution)/shard_map/pallas_call | solution.py:291
  26.2 0.0 copy-done
  26.2 0.6 %fusion = f32[1,2,4096]{2,1,0:T(2,128)} fusion(f32[2,4096]{1,0:T(2,128)S(1)} %shard_map.55, bf16[1,2,4096]{2,1,0:T(2,128)(2,1)S(1)} %copy-done), kind=kLoop, calls=%fused_computation.1 | loop fusion | flops 16384 | bytes 81920 | tf_op jit(solution)/shard_map/broadcast_in_dim | solution.py:316
Async XLA Ops:
  0.0 26.2 %copy-start = (bf16[1,2,4096]{2,1,0:T(2,128)(2,1)S(1)}, bf16[1,2,4096]{2,1,0:T(2,128)(2,1)}, u32[]{:S(2)}) copy-start(bf16[1,2,4096]{2,1,0:T(2,128)(2,1)} %param.6) | copy-start | bytes 49156

commit v3 on v2

--- a/solution.py
+++ b/solution.py
@@ -14,8 +14,10 @@
 LANES = 128
 GROUPS = SIDE * SIDE
 SIZE = 2 * GROUPS
-OWNERS = ((0, 1), (1, 0), (2, 0), (3, 0), (4, 0), (5, 0), (6, 0), (7, 0))
+OWNERS = ((0, 1), (1, 0), (2, 0), (3, 0), (0, 2), (5, 0), (6, 0), (7, 0))
 BLOCKS = len(OWNERS) * CORES
+QUARTER = SIDE // 4
+HALF = GROUPS // 2
 
 
 def parts_of(value):
@@ -68,12 +70,14 @@
 
 
 def slot_of(group):
-    return lax.rem(group, 2) * (GROUPS // 2) + lax.div(group, 2)
+    y, z = lax.div(group, SIDE), lax.rem(group, SIDE)
+    late, rest = lax.div(z, SIDE // 2), lax.rem(z, SIDE // 2)
+    return ((late * 2 + lax.rem(rest, 2)) * QUARTER + lax.div(rest, 2)) * SIDE + y
 
 
 def kernel(
     sino_any, bank_any, index_any, taps_any, out_ref,
-    sino_ref, bank_ref, index_ref, taps_ref, send_buf, leaf_buf, result_buf, image_buf, tree_buf,
+    sino_ref, bank_ref, index_ref, taps_ref, send_buf, leaf_buf, result_buf, image_buf, tree_buf, early_buf,
     local_sem, leaf_send, leaf_recv, image_send, image_recv,
 ):
     views, columns = sino_ref.shape
@@ -87,20 +91,25 @@
     here = [group == y * SIDE + z for y, z in OWNERS]
     is_owner = functools.reduce(jnp.logical_or, here)
     mine = core + sum(jnp.where(hit, CORES * i, 0) for i, hit in enumerate(here))
-    half = GROUPS // 2
+    late = lax.div(lax.rem(group, SIDE), SIDE // 2)
 
     has_side = [first > 0, True, True, first + CORES < slices]
     side_cut = [lax.rem(first + side - 1 + slices, slices) for side in range(4)]
 
     barrier = pltpu.get_barrier_semaphore()
-    sino_copy = pltpu.make_async_copy(sino_any, sino_ref, local_sem.at[0])
-    sino_copy.start()
+    parts = [pl.ds(p * (columns // 2), columns // 2) for p in range(2)]
+    sino_copies = [
+        pltpu.make_async_copy(sino_any.at[:, part], sino_ref.at[:, part], local_sem.at[p])
+        for p, part in enumerate(parts)
+    ]
+    for copy in sino_copies:
+        copy.start()
 
     @pl.when(is_owner)
     def _():
-        bank_copy = pltpu.make_async_copy(bank_any, bank_ref, local_sem.at[1])
-        index_copy = pltpu.make_async_copy(index_any, index_ref, local_sem.at[2])
-        taps_copy = pltpu.make_async_copy(taps_any, taps_ref, local_sem.at[3])
+        bank_copy = pltpu.make_async_copy(bank_any, bank_ref, local_sem.at[2])
+        index_copy = pltpu.make_async_copy(index_any, index_ref, local_sem.at[3])
+        taps_copy = pltpu.make_async_copy(taps_any, taps_ref, local_sem.at[4])
         bank_copy.start()
         index_copy.start()
         taps_copy.start()
@@ -125,95 +134,127 @@
         index_copy.wait()
         taps_copy.wait()
 
-    sino_copy.wait()
-    total = jnp.sum(sino_ref[...].astype(jnp.float32), axis=0, keepdims=True)
     margin = jnp.zeros((1, LANES // 2), jnp.float32)
-    total = jnp.concatenate([margin, total, margin], axis=1)
-    for b in range(BLOCKS):
-        for c in range(window):
-            start = (b * per_block + c) * LANES
-            send_buf[b, c : c + 1, :] = total[:, start : start + LANES]
-
-    other = jnp.where(core == 0, cut - 1, cut + 1)
+    pending = margin
+    row = 0
+    for part, copy in zip(parts, sino_copies):
+        copy.wait()
+        total = jnp.sum(sino_ref[:, part].astype(jnp.float32), axis=0, keepdims=True)
+        if part is parts[-1]:
+            total = jnp.concatenate([total, margin], axis=1)
+        total = jnp.concatenate([pending, total], axis=1)
+        for c in range(total.shape[1] // LANES):
+            for b in range(BLOCKS):
+                if 0 <= row - b * per_block < window:
+                    send_buf[b, row - b * per_block : row - b * per_block + 1, :] = total[:, c * LANES : (c + 1) * LANES]
+            row += 1
+        pending = total[:, total.shape[1] // LANES * LANES :]
+
     has_other = jnp.where(core == 0, cut > 0, cut < slices - 1)
     other_first = lax.rem(jnp.where(core == 0, cut - CORES, cut + 1) + slices, slices)
     other_side = jnp.where(core == 0, 3, 0)
     n_owners = BLOCKS + jnp.where(has_other, BLOCKS, 0) - jnp.where(is_owner, 1, 0)
     pl.semaphore_wait(barrier, n_owners)
 
-    def leaf_copy(b, plane):
-        base, side = (first, 1 + core) if plane == 0 else (other_first, other_side)
+    def leaf_copy(b, turn):
+        own = core != turn
+        side = jnp.where(own, 1 + core, other_side)
+        y, z = OWNERS[b // CORES]
         return pltpu.make_async_remote_copy(
             src_ref=send_buf.at[b],
             dst_ref=leaf_buf.at[side, slot_of(group)],
             send_sem=leaf_send,
-            recv_sem=leaf_recv.at[side],
-            device_id=(OWNERS[b // CORES][0] * SIDE + OWNERS[b // CORES][1], base + b % CORES),
+            recv_sem=leaf_recv.at[side, late],
+            device_id=(y * SIDE + z, jnp.where(own, first, other_first) + b % CORES),
             device_id_type=MESH,
         )
 
-    def each_leaf(act):
-        for plane in range(2):
+    for turn in range(2):
+        valid = jnp.where(core != turn, True, has_other)
+
+        @pl.when(jnp.logical_and(valid, jnp.logical_not(is_owner)))
+        def _():
             for b in range(BLOCKS):
-                valid = has_other
-                if plane == 0:
-                    valid = jnp.logical_not(jnp.logical_and(is_owner, mine == b))
-
-                @pl.when(valid)
+                leaf_copy(b, turn).start()
+
+        @pl.when(jnp.logical_and(valid, is_owner))
+        def _():
+            for b in range(BLOCKS):
+
+                @pl.when(jnp.logical_or(core == turn, mine != b))
                 def _():
-                    act(leaf_copy(b, plane))
-
-    each_leaf(lambda copy: copy.start())
+                    leaf_copy(b, turn).start()
+
+    def all_left(count):
+        sent = send_buf.at[pl.ds(0, count)]
+        pltpu.make_async_copy(sent, sent, leaf_send).wait()
+
+    pl.when(is_owner)(lambda: all_left(BLOCKS - 1))
+    pl.when(jnp.logical_not(is_owner))(lambda: all_left(BLOCKS))
+    pl.when(has_other)(lambda: all_left(BLOCKS))
 
     @pl.when(is_owner)
     def _():
         leaf_buf[1 + core, slot_of(group)] = send_buf[mine]
         row, col = iota((SIZE, SIZE), 0), iota((SIZE, SIZE), 1)
-        natural = 4 * (col % half) + 2 * (col % GROUPS // half) + col // GROUPS
+        place = lax.rem(col, HALF)
+        z = (
+            col // GROUPS * (SIDE // 2)
+            + lax.rem(place // SIDE, QUARTER) * 2
+            + place // (SIDE * QUARTER)
+        )
+        natural = 2 * (lax.rem(place, SIDE) * SIDE + z) + lax.rem(col // HALF, 2)
         order = (row == natural).astype(jnp.bfloat16)
         tree = tree_matrix(bank_ref, index_ref) * (1.0 / math.sqrt(views))
         high, low = [
             jnp.dot(part, order, preferred_element_type=jnp.float32).astype(jnp.bfloat16) for part in parts_of(tree)
         ]
-        tree_buf[...] = jnp.concatenate([high, low, high], axis=1)
-
-        for side in range(4):
-            def wait(count):
-                done = leaf_buf.at[side, pl.ds(0, count)]
-                pltpu.make_async_copy(done, done, leaf_recv.at[side]).wait()
-
-            if side in (1, 2):
-                own = core == side - 1
-                pl.when(own)(lambda: wait(GROUPS - 1))
-                pl.when(jnp.logical_not(own))(lambda: wait(GROUPS))
-            else:
-                pl.when(has_side[side])(lambda: wait(GROUPS))
-
-        lane, place = iota((half, LANES), 1), iota((half, LANES), 0)
-        moved = [half // 2 - 1 - place, place - half // 2]
-        back = lax.rem(lane - moved[0] + LANES // 2 + LANES, LANES)
-        leaves = []
-        for e in range(CORES):
-            mixed = [[None] * 2 for _ in range(window)]
-            for c in range(window):
-                term = None
-                for tap in range(3):
-                    value = taps_ref[tap] * leaf_buf[e + tap, :, c, :]
-                    if e + tap in (0, 3):
-                        value = jnp.where(has_side[e + tap], value, 0.0)
-                    term = value if term is None else term + value
-                mixed[c] = [term[:half], term[half:]]
-            rows = []
-            for r in range(2):
-                for h in range(2):
+        for part in range(2):
+            span = slice(part * GROUPS, (part + 1) * GROUPS)
+            tree_buf[part] = jnp.concatenate([high[:, span], low[:, span], high[:, span]], axis=1)
+
+        lane, place = iota((HALF, LANES), 1), iota((HALF, LANES), 0)
+        image = None
+        for part in range(2):
+            for side in range(4):
+                def wait(count):
+                    done = leaf_buf.at[side, pl.ds(0, count)]
+                    pltpu.make_async_copy(done, done, leaf_recv.at[side, part]).wait()
+
+                if side in (1, 2) and part == 0:
+                    own = core == side - 1
+                    pl.when(own)(lambda: wait(HALF - 1))
+                    pl.when(jnp.logical_not(own))(lambda: wait(HALF))
+                else:
+                    pl.when(has_side[side])(lambda: wait(HALF))
+
+            pair = lax.rem(place, SIDE) * (SIDE // 2) + lax.rem(place // SIDE, QUARTER) + part * QUARTER
+            moved = [GROUPS // 4 - 1 - pair, pair - GROUPS // 4]
+            back = lax.rem(lane - moved[0] + LANES // 2 + LANES, LANES)
+            leaves = []
+            for e in range(CORES):
+                mixed = []
+                for c in range(window):
+                    term = None
+                    for tap in range(3):
+                        value = taps_ref[tap] * leaf_buf[e + tap, part * HALF : (part + 1) * HALF, c, :]
+                        if e + tap in (0, 3):
+                            value = jnp.where(has_side[e + tap], value, 0.0)
+                        term = value if term is None else term + value
+                    mixed.append(term)
+                rows = []
+                for r in range(2):
                     turned = []
                     for c in range(window):
-                        if r == 1:
-                            turned.append(
-                                pltpu.roll(mixed[c][h], LANES // 2 - half // 2, 1, stride=1, stride_axis=0)
-                            )
-                        else:
-                            turned.append(jnp.take_along_axis(mixed[c][h], back, axis=1))
+                        if r == 0:
+                            turned.append(jnp.take_along_axis(mixed[c], back, axis=1))
+                            continue
+                        pieces = []
+                        for k in range(HALF // SIDE):
+                            base = LANES // 2 - GROUPS // 4 + part * QUARTER + k % QUARTER
+                            piece = mixed[c][k * SIDE : (k + 1) * SIDE]
+                            pieces.append(pltpu.roll(piece, base, 1, stride=SIDE // 2, stride_axis=0))
+                        turned.append(jnp.concatenate(pieces, axis=0))
                     rows.append(
                         jnp.concatenate(
                             [
@@ -223,11 +264,15 @@
                             axis=1,
                         )
                     )
-            leaves.append(jnp.concatenate(rows, axis=0))
-        high, low = parts_of(jnp.concatenate(leaves, axis=1))
-        image = jnp.dot(
-            tree_buf[...], jnp.concatenate([high, high, low], axis=0), preferred_element_type=jnp.float32
-        )
+                leaves.append(jnp.concatenate(rows, axis=0))
+            high, low = parts_of(jnp.concatenate(leaves, axis=1))
+            product = jnp.dot(
+                tree_buf[part], jnp.concatenate([high, high, low], axis=0), preferred_element_type=jnp.float32
+            )
+            if part == 0:
+                early_buf[...] = product
+            else:
+                image = early_buf[...] + product
         for e in range(CORES):
             for i in range(per_block):
                 start = (e * per_block + i) * LANES
@@ -266,8 +311,6 @@
         for i in range(per_block):
             c = b * per_block + i
             out_ref[:, c * LANES : (c + 1) * LANES] = image_buf[2 * b : 2 * b + 2, i, :]
-
-    each_leaf(lambda copy: copy.wait_send())
 
     @pl.when(is_owner)
     def _():
@@ -302,10 +345,11 @@
             pltpu.VMEM((4, GROUPS, per_block + 1, LANES), jnp.float32),
             pltpu.VMEM((CORES, SIZE, per_block, LANES), jnp.float32),
             pltpu.VMEM((2 * BLOCKS, per_block, LANES), jnp.float32),
-            pltpu.VMEM((SIZE, 3 * SIZE), jnp.bfloat16),
-            pltpu.SemaphoreType.DMA((4,)),
+            pltpu.VMEM((2, SIZE, 3 * GROUPS), jnp.bfloat16),
+            pltpu.VMEM((SIZE, CORES * columns // BLOCKS), jnp.float32),
+            pltpu.SemaphoreType.DMA((5,)),
             pltpu.SemaphoreType.DMA,
-            pltpu.SemaphoreType.DMA((4,)),
+            pltpu.SemaphoreType.DMA((4, 2)),
             pltpu.SemaphoreType.DMA,
             pltpu.SemaphoreType.DMA,
         ],

time: 27 us -> 25.6 us (0.948)
  Pallas kernels: 26.1 us -> 24.8 us
    pallas_call x1, Pallas kernels: 26.1 us -> 24.8 us  [shards(): pl.pallas_call(kernel, out_shape=pltpu.VMEM((2, columns), jnp.float32), i...]
where the time goes in v3:
time: 25.6 us; the launch traced here: 25.5 us
  Pallas kernels  24.8 us (97%)
  other arithmetic  0.63 us (2%)
    pallas_call x1, Pallas kernels, shards(): pl.pallas_call(kernel, out_shape=pltpu.VMEM((2, columns), jnp.float32), i...  24.8 us
    broadcast_in_dim x1, other arithmetic, shards(): return (estimate[0].astype(jnp.float32) - mixed)[None]  0.63 us

profile of v3, /device:TPU:1, one launch (start us, length us, event | category | flops | bytes accessed | tf_op | source)
XLA Modules:
  0.0 25.5 jit_solution(7042684432454754095)
XLA Ops:
  0.0 0.0 copy-start
  0.0 24.8 %shard_map.55 = f32[2,4096]{1,0:T(2,128)S(1)} custom-call(bf16[12,4096]{1,0:T(8,128)(2,1)} %bitcast.8, f32[4,64,128]{2,1,0:T(8,128)} %bitcast.9, s32[1,128]{1,0:T(1,128)} %bitcast.10, f32[3]{0:T(128)} %taps_any.1), custom_call_target="tpu_custom_call" | custom-call | tf_op jit(solution)/shard_map/pallas_call | solution.py:334
  24.8 0.0 copy-done
  24.8 0.6 %fusion = f32[1,2,4096]{2,1,0:T(2,128)} fusion(f32[2,4096]{1,0:T(2,128)S(1)} %shard_map.55, bf16[1,2,4096]{2,1,0:T(2,128)(2,1)S(1)} %copy-done), kind=kLoop, calls=%fused_computation.1 | loop fusion | flops 16384 | bytes 81920 | tf_op jit(solution)/shard_map/broadcast_in_dim | solution.py:360
Async XLA Ops:
  0.0 24.8 %copy-start = (bf16[1,2,4096]{2,1,0:T(2,128)(2,1)S(1)}, bf16[1,2,4096]{2,1,0:T(2,128)(2,1)}, u32[]{:S(2)}) copy-start(bf16[1,2,4096]{2,1,0:T(2,128)(2,1)} %param.6) | copy-start | bytes 49156

commit v4 on v3

--- a/solution.py
+++ b/solution.py
@@ -14,8 +14,8 @@
 LANES = 128
 GROUPS = SIDE * SIDE
 SIZE = 2 * GROUPS
-OWNERS = ((0, 1), (1, 0), (2, 0), (3, 0), (0, 2), (5, 0), (6, 0), (7, 0))
-BLOCKS = len(OWNERS) * CORES
+OWNERS = ((1, 0, 0), (1, 1, 1), (1, 1, 0), (2, 0, 0), (2, 0, 1), (7, 0, 0), (7, 0, 1), (6, 0, 0), (6, 0, 1), (3, 0, 0), (3, 0, 1), (5, 0, 0), (5, 0, 1), (0, 1, 0), (0, 1, 1), (4, 0, 0))
+BLOCKS = len(OWNERS)
 QUARTER = SIDE // 4
 HALF = GROUPS // 2
 
@@ -88,9 +88,9 @@
     cut = lax.axis_index("cuts")
     core = lax.rem(cut, CORES)
     first = cut - core
-    here = [group == y * SIDE + z for y, z in OWNERS]
+    here = [jnp.logical_and(group == y * SIDE + z, core == c) for y, z, c in OWNERS]
     is_owner = functools.reduce(jnp.logical_or, here)
-    mine = core + sum(jnp.where(hit, CORES * i, 0) for i, hit in enumerate(here))
+    mine = sum(jnp.where(hit, b, 0) for b, hit in enumerate(here))
     late = lax.div(lax.rem(group, SIDE), SIDE // 2)
 
     has_side = [first > 0, True, True, first + CORES < slices]
@@ -159,13 +159,13 @@
     def leaf_copy(b, turn):
         own = core != turn
         side = jnp.where(own, 1 + core, other_side)
-        y, z = OWNERS[b // CORES]
+        y, z, c = OWNERS[b]
         return pltpu.make_async_remote_copy(
             src_ref=send_buf.at[b],
             dst_ref=leaf_buf.at[side, slot_of(group)],
             send_sem=leaf_send,
             recv_sem=leaf_recv.at[side, late],
-            device_id=(y * SIDE + z, jnp.where(own, first, other_first) + b % CORES),
+            device_id=(y * SIDE + z, jnp.where(own, first, other_first) + c),
             device_id_type=MESH,
         )
 
@@ -292,7 +292,7 @@
                         src_ref=result_buf.at[e, pl.ds(2 * target, 2)],
                         dst_ref=image_buf.at[pl.ds(2 * mine, 2)],
                         send_sem=image_send,
-                        recv_sem=image_recv,
+                        recv_sem=image_recv.at[mine],
                         device_id=(target, first + e),
                         device_id_type=MESH,
                     ).start()
@@ -300,14 +300,14 @@
             return carry
 
         lax.fori_loop(0, GROUPS, give, 0)
-        got = image_buf.at[pl.ds(0, 2 * (BLOCKS - 1))]
-        pltpu.make_async_copy(got, got, image_recv).wait()
-
-    @pl.when(jnp.logical_not(is_owner))
-    def _():
-        pltpu.make_async_copy(image_buf, image_buf, image_recv).wait()
 
     for b in range(BLOCKS):
+        got = image_buf.at[pl.ds(2 * b, 2)]
+
+        @pl.when(jnp.logical_not(jnp.logical_and(is_owner, mine == b)))
+        def _():
+            pltpu.make_async_copy(got, got, image_recv.at[b]).wait()
+
         for i in range(per_block):
             c = b * per_block + i
             out_ref[:, c * LANES : (c + 1) * LANES] = image_buf[2 * b : 2 * b + 2, i, :]
@@ -351,7 +351,7 @@
             pltpu.SemaphoreType.DMA,
             pltpu.SemaphoreType.DMA((4, 2)),
             pltpu.SemaphoreType.DMA,
-            pltpu.SemaphoreType.DMA,
+            pltpu.SemaphoreType.DMA((BLOCKS,)),
         ],
         compiler_params=pltpu.CompilerParams(
             collective_id=0, has_side_effects=True, vmem_limit_bytes=32 * 1024 * 1024

time: 25.6 us -> 25.5 us (level)
  no operation moved by 1% of the time
where the time goes in v4:
time: 25.5 us; the launch traced here: 25.3 us
  Pallas kernels  24.7 us (97%)
  other arithmetic  0.63 us (2%)
    pallas_call x1, Pallas kernels, shards(): pl.pallas_call(kernel, out_shape=pltpu.VMEM((2, columns), jnp.float32), i...  24.7 us
    broadcast_in_dim x1, other arithmetic, shards(): return (estimate[0].astype(jnp.float32) - mixed)[None]  0.63 us

profile of v4, /device:TPU:1, one launch (start us, length us, event | category | flops | bytes accessed | tf_op | source)
XLA Modules:
  0.0 25.3 jit_solution(7700393561971575770)
XLA Ops:
  0.0 0.0 copy-start
  0.0 24.7 %shard_map.55 = f32[2,4096]{1,0:T(2,128)S(1)} custom-call(bf16[12,4096]{1,0:T(8,128)(2,1)} %bitcast.8, f32[4,64,128]{2,1,0:T(8,128)} %bitcast.9, s32[1,128]{1,0:T(1,128)} %bitcast.10, f32[3]{0:T(128)} %taps_any.1), custom_call_target="tpu_custom_call" | custom-call | tf_op jit(solution)/shard_map/pallas_call | solution.py:334
  24.7 0.0 copy-done
  24.7 0.6 %fusion = f32[1,2,4096]{2,1,0:T(2,128)} fusion(f32[2,4096]{1,0:T(2,128)S(1)} %shard_map.55, bf16[1,2,4096]{2,1,0:T(2,128)(2,1)S(1)} %copy-done), kind=kLoop, calls=%fused_computation.1 | loop fusion | flops 16384 | bytes 81920 | tf_op jit(solution)/shard_map/broadcast_in_dim | solution.py:360
Async XLA Ops:
  0.0 24.7 %copy-start = (bf16[1,2,4096]{2,1,0:T(2,128)(2,1)S(1)}, bf16[1,2,4096]{2,1,0:T(2,128)(2,1)}, u32[]{:S(2)}) copy-start(bf16[1,2,4096]{2,1,0:T(2,128)(2,1)} %param.6) | copy-start | bytes 49156

commit v5 on v4

--- a/solution.py
+++ b/solution.py
@@ -16,6 +16,7 @@
 SIZE = 2 * GROUPS
 OWNERS = ((1, 0, 0), (1, 1, 1), (1, 1, 0), (2, 0, 0), (2, 0, 1), (7, 0, 0), (7, 0, 1), (6, 0, 0), (6, 0, 1), (3, 0, 0), (3, 0, 1), (5, 0, 0), (5, 0, 1), (0, 1, 0), (0, 1, 1), (4, 0, 0))
 BLOCKS = len(OWNERS)
+AHEAD = 2 * SIDE
 QUARTER = SIDE // 4
 HALF = GROUPS // 2
 
@@ -214,92 +215,98 @@
             tree_buf[part] = jnp.concatenate([high[:, span], low[:, span], high[:, span]], axis=1)
 
         lane, place = iota((HALF, LANES), 1), iota((HALF, LANES), 0)
-        image = None
-        for part in range(2):
-            for side in range(4):
-                def wait(count):
-                    done = leaf_buf.at[side, pl.ds(0, count)]
-                    pltpu.make_async_copy(done, done, leaf_recv.at[side, part]).wait()
-
-                if side in (1, 2) and part == 0:
-                    own = core == side - 1
-                    pl.when(own)(lambda: wait(HALF - 1))
-                    pl.when(jnp.logical_not(own))(lambda: wait(HALF))
-                else:
-                    pl.when(has_side[side])(lambda: wait(HALF))
-
+
+        def arrived(side, part):
+            def wait(count):
+                done = leaf_buf.at[side, pl.ds(0, count)]
+                pltpu.make_async_copy(done, done, leaf_recv.at[side, part]).wait()
+
+            if side in (1, 2) and part == 0:
+                own = core == side - 1
+                pl.when(own)(lambda: wait(HALF - 1))
+                pl.when(jnp.logical_not(own))(lambda: wait(HALF))
+            else:
+                pl.when(has_side[side])(lambda: wait(HALF))
+
+        def merged(part, terms):
             pair = lax.rem(place, SIDE) * (SIDE // 2) + lax.rem(place // SIDE, QUARTER) + part * QUARTER
             moved = [GROUPS // 4 - 1 - pair, pair - GROUPS // 4]
             back = lax.rem(lane - moved[0] + LANES // 2 + LANES, LANES)
-            leaves = []
-            for e in range(CORES):
-                mixed = []
+            mixed = []
+            for c in range(window):
+                total = None
+                for tap, side in terms:
+                    value = taps_ref[tap] * leaf_buf[side, part * HALF : (part + 1) * HALF, c, :]
+                    if side in (0, 3):
+                        value = jnp.where(has_side[side], value, 0.0)
+                    total = value if total is None else total + value
+                mixed.append(total)
+            rows = []
+            for r in range(2):
+                turned = []
                 for c in range(window):
-                    term = None
-                    for tap in range(3):
-                        value = taps_ref[tap] * leaf_buf[e + tap, part * HALF : (part + 1) * HALF, c, :]
-                        if e + tap in (0, 3):
-                            value = jnp.where(has_side[e + tap], value, 0.0)
-                        term = value if term is None else term + value
-                    mixed.append(term)
-                rows = []
-                for r in range(2):
-                    turned = []
-                    for c in range(window):
-                        if r == 0:
-                            turned.append(jnp.take_along_axis(mixed[c], back, axis=1))
-                            continue
-                        pieces = []
-                        for k in range(HALF // SIDE):
-                            base = LANES // 2 - GROUPS // 4 + part * QUARTER + k % QUARTER
-                            piece = mixed[c][k * SIDE : (k + 1) * SIDE]
-                            pieces.append(pltpu.roll(piece, base, 1, stride=SIDE // 2, stride_axis=0))
-                        turned.append(jnp.concatenate(pieces, axis=0))
-                    rows.append(
-                        jnp.concatenate(
-                            [
-                                jnp.where(lane - moved[r] < LANES // 2, turned[i], turned[i + 1])
-                                for i in range(per_block)
-                            ],
-                            axis=1,
-                        )
+                    if r == 0:
+                        turned.append(jnp.take_along_axis(mixed[c], back, axis=1))
+                        continue
+                    pieces = []
+                    for k in range(HALF // SIDE):
+                        base = LANES // 2 - GROUPS // 4 + part * QUARTER + k % QUARTER
+                        piece = mixed[c][k * SIDE : (k + 1) * SIDE]
+                        pieces.append(pltpu.roll(piece, base, 1, stride=SIDE // 2, stride_axis=0))
+                    turned.append(jnp.concatenate(pieces, axis=0))
+                rows.append(
+                    jnp.concatenate(
+                        [jnp.where(lane - moved[r] < LANES // 2, turned[i], turned[i + 1]) for i in range(per_block)],
+                        axis=1,
                     )
-                leaves.append(jnp.concatenate(rows, axis=0))
-            high, low = parts_of(jnp.concatenate(leaves, axis=1))
-            product = jnp.dot(
+                )
+            high, low = parts_of(jnp.concatenate(rows, axis=0))
+            return jnp.dot(
                 tree_buf[part], jnp.concatenate([high, high, low], axis=0), preferred_element_type=jnp.float32
             )
-            if part == 0:
-                early_buf[...] = product
-            else:
-                image = early_buf[...] + product
-        for e in range(CORES):
+
+        def keep(e, image):
             for i in range(per_block):
-                start = (e * per_block + i) * LANES
-                result_buf[e, :, i, :] = image[:, start : start + LANES]
-
-        image_buf[pl.ds(2 * mine, 2)] = result_buf[core, pl.ds(2 * group, 2)]
-
-        def give(step, carry):
+                result_buf[e, :, i, :] = image[:, i * LANES : (i + 1) * LANES]
+
+        def give(e, step):
             turn = lax.rem(step, SIDE)
             y = jnp.where(turn < SIDE // 2, turn, SIDE + SIDE // 2 - 1 - turn)
             target = y * SIDE + lax.div(step, SIDE)
-            for e in range(CORES):
-
-                @pl.when(jnp.logical_or(target != group, core != e))
-                def _():
-                    pltpu.make_async_remote_copy(
-                        src_ref=result_buf.at[e, pl.ds(2 * target, 2)],
-                        dst_ref=image_buf.at[pl.ds(2 * mine, 2)],
-                        send_sem=image_send,
-                        recv_sem=image_recv.at[mine],
-                        device_id=(target, first + e),
-                        device_id_type=MESH,
-                    ).start()
-
-            return carry
-
-        lax.fori_loop(0, GROUPS, give, 0)
+
+            @pl.when(jnp.logical_or(target != group, core != e))
+            def _():
+                pltpu.make_async_remote_copy(
+                    src_ref=result_buf.at[e, pl.ds(2 * target, 2)],
+                    dst_ref=image_buf.at[pl.ds(2 * mine, 2)],
+                    send_sem=image_send,
+                    recv_sem=image_recv.at[mine],
+                    device_id=(target, first + e),
+                    device_id_type=MESH,
+                ).start()
+
+        def give_all(start, stop, which):
+            def body(step, carry):
+                for e in which:
+                    give(e, step)
+                return carry
+
+            lax.fori_loop(start, stop, body, 0)
+
+        for side in range(4):
+            arrived(side, 0)
+        early_buf[0] = merged(0, [(0, 0), (1, 1), (2, 2)])
+        early_buf[1] = merged(0, [(0, 1), (1, 2), (2, 3)])
+        for side in range(3):
+            arrived(side, 1)
+        keep(0, early_buf[0] + merged(1, [(0, 0), (1, 1), (2, 2)]))
+        give_all(0, AHEAD, (0,))
+        early_buf[1] += merged(1, [(0, 1), (1, 2)])
+        arrived(3, 1)
+        keep(1, early_buf[1] + merged(1, [(2, 3)]))
+        give_all(0, AHEAD, (1,))
+        give_all(AHEAD, GROUPS, (0, 1))
+        image_buf[pl.ds(2 * mine, 2)] = result_buf[core, pl.ds(2 * group, 2)]
 
     for b in range(BLOCKS):
         got = image_buf.at[pl.ds(2 * b, 2)]
@@ -346,7 +353,7 @@
             pltpu.VMEM((CORES, SIZE, per_block, LANES), jnp.float32),
             pltpu.VMEM((2 * BLOCKS, per_block, LANES), jnp.float32),
             pltpu.VMEM((2, SIZE, 3 * GROUPS), jnp.bfloat16),
-            pltpu.VMEM((SIZE, CORES * columns // BLOCKS), jnp.float32),
+            pltpu.VMEM((CORES, SIZE, columns // BLOCKS), jnp.float32),
             pltpu.SemaphoreType.DMA((5,)),
             pltpu.SemaphoreType.DMA,
             pltpu.SemaphoreType.DMA((4, 2)),

time: 25.5 us -> 25.1 us (0.984)
  Pallas kernels: 24.7 us -> 24.2 us
    pallas_call x1, Pallas kernels: 24.7 us -> 24.2 us  [shards(): pl.pallas_call(kernel, out_shape=pltpu.VMEM((2, columns), jnp.float32), i...]
where the time goes in v5:
time: 25.1 us; the launch traced here: 24.9 us
  Pallas kernels  24.2 us (96%)
  other arithmetic  0.63 us (3%)
    pallas_call x1, Pallas kernels, shards(): pl.pallas_call(kernel, out_shape=pltpu.VMEM((2, columns), jnp.float32), i...  24.2 us
    broadcast_in_dim x1, other arithmetic, shards(): return (estimate[0].astype(jnp.float32) - mixed)[None]  0.63 us

profile of v5, /device:TPU:1, one launch (start us, length us, event | category | flops | bytes accessed | tf_op | source)
XLA Modules:
  0.0 24.9 jit_solution(8820549305430837753)
XLA Ops:
  0.0 0.0 copy-start
  0.0 24.2 %shard_map.55 = f32[2,4096]{1,0:T(2,128)S(1)} custom-call(bf16[12,4096]{1,0:T(8,128)(2,1)} %bitcast.8, f32[4,64,128]{2,1,0:T(8,128)} %bitcast.9, s32[1,128]{1,0:T(1,128)} %bitcast.10, f32[3]{0:T(128)} %taps_any.1), custom_call_target="tpu_custom_call" | custom-call | tf_op jit(solution)/shard_map/pallas_call | solution.py:341
  24.2 0.0 copy-done
  24.2 0.6 %fusion = f32[1,2,4096]{2,1,0:T(2,128)} fusion(f32[2,4096]{1,0:T(2,128)S(1)} %shard_map.55, bf16[1,2,4096]{2,1,0:T(2,128)(2,1)S(1)} %copy-done), kind=kLoop, calls=%fused_computation.1 | loop fusion | flops 16384 | bytes 81920 | tf_op jit(solution)/shard_map/broadcast_in_dim | solution.py:367
Async XLA Ops:
  0.0 24.2 %copy-start = (bf16[1,2,4096]{2,1,0:T(2,128)(2,1)S(1)}, bf16[1,2,4096]{2,1,0:T(2,128)(2,1)}, u32[]{:S(2)}) copy-start(bf16[1,2,4096]{2,1,0:T(2,128)(2,1)} %param.6) | copy-start | bytes 49156

commit v6 on v5

--- a/solution.py
+++ b/solution.py
@@ -14,9 +14,9 @@
 LANES = 128
 GROUPS = SIDE * SIDE
 SIZE = 2 * GROUPS
-OWNERS = ((1, 0, 0), (1, 1, 1), (1, 1, 0), (2, 0, 0), (2, 0, 1), (7, 0, 0), (7, 0, 1), (6, 0, 0), (6, 0, 1), (3, 0, 0), (3, 0, 1), (5, 0, 0), (5, 0, 1), (0, 1, 0), (0, 1, 1), (4, 0, 0))
+OWNERS = ((0, 1, 0), (0, 1, 1), (1, 1, 0), (1, 1, 1), (4, 0, 0), (1, 0, 0), (2, 0, 0), (2, 0, 1), (7, 0, 0), (7, 0, 1), (6, 0, 0), (6, 0, 1), (3, 0, 0), (3, 0, 1), (5, 0, 0), (5, 0, 1))
 BLOCKS = len(OWNERS)
-AHEAD = 2 * SIDE
+AHEAD, LEAD = 10, 2
 QUARTER = SIDE // 4
 HALF = GROUPS // 2
 
@@ -98,19 +98,14 @@
     side_cut = [lax.rem(first + side - 1 + slices, slices) for side in range(4)]
 
     barrier = pltpu.get_barrier_semaphore()
-    parts = [pl.ds(p * (columns // 2), columns // 2) for p in range(2)]
-    sino_copies = [
-        pltpu.make_async_copy(sino_any.at[:, part], sino_ref.at[:, part], local_sem.at[p])
-        for p, part in enumerate(parts)
-    ]
-    for copy in sino_copies:
-        copy.start()
+    sino_copy = pltpu.make_async_copy(sino_any, sino_ref, local_sem.at[0])
+    sino_copy.start()
 
     @pl.when(is_owner)
     def _():
-        bank_copy = pltpu.make_async_copy(bank_any, bank_ref, local_sem.at[2])
-        index_copy = pltpu.make_async_copy(index_any, index_ref, local_sem.at[3])
-        taps_copy = pltpu.make_async_copy(taps_any, taps_ref, local_sem.at[4])
+        bank_copy = pltpu.make_async_copy(bank_any, bank_ref, local_sem.at[1])
+        index_copy = pltpu.make_async_copy(index_any, index_ref, local_sem.at[2])
+        taps_copy = pltpu.make_async_copy(taps_any, taps_ref, local_sem.at[3])
         bank_copy.start()
         index_copy.start()
         taps_copy.start()
@@ -135,21 +130,14 @@
         index_copy.wait()
         taps_copy.wait()
 
+    sino_copy.wait()
+    total = jnp.sum(sino_ref[...].astype(jnp.float32), axis=0, keepdims=True)
     margin = jnp.zeros((1, LANES // 2), jnp.float32)
-    pending = margin
-    row = 0
-    for part, copy in zip(parts, sino_copies):
-        copy.wait()
-        total = jnp.sum(sino_ref[:, part].astype(jnp.float32), axis=0, keepdims=True)
-        if part is parts[-1]:
-            total = jnp.concatenate([total, margin], axis=1)
-        total = jnp.concatenate([pending, total], axis=1)
-        for c in range(total.shape[1] // LANES):
-            for b in range(BLOCKS):
-                if 0 <= row - b * per_block < window:
-                    send_buf[b, row - b * per_block : row - b * per_block + 1, :] = total[:, c * LANES : (c + 1) * LANES]
-            row += 1
-        pending = total[:, total.shape[1] // LANES * LANES :]
+    total = jnp.concatenate([margin, total, margin], axis=1)
+    for b in range(BLOCKS):
+        for c in range(window):
+            start = (b * per_block + c) * LANES
+            send_buf[b, c : c + 1, :] = total[:, start : start + LANES]
 
     has_other = jnp.where(core == 0, cut > 0, cut < slices - 1)
     other_first = lax.rem(jnp.where(core == 0, cut - CORES, cut + 1) + slices, slices)
@@ -304,8 +292,15 @@
         early_buf[1] += merged(1, [(0, 1), (1, 2)])
         arrived(3, 1)
         keep(1, early_buf[1] + merged(1, [(2, 3)]))
-        give_all(0, AHEAD, (1,))
-        give_all(AHEAD, GROUPS, (0, 1))
+        give_all(0, AHEAD + LEAD, (1,))
+
+        def give_both(step, carry):
+            give(0, step)
+            give(1, step + LEAD)
+            return carry
+
+        lax.fori_loop(AHEAD, GROUPS - LEAD, give_both, 0)
+        give_all(GROUPS - LEAD, GROUPS, (0,))
         image_buf[pl.ds(2 * mine, 2)] = result_buf[core, pl.ds(2 * group, 2)]
 
     for b in range(BLOCKS):
@@ -354,7 +349,7 @@
             pltpu.VMEM((2 * BLOCKS, per_block, LANES), jnp.float32),
             pltpu.VMEM((2, SIZE, 3 * GROUPS), jnp.bfloat16),
             pltpu.VMEM((CORES, SIZE, columns // BLOCKS), jnp.float32),
-            pltpu.SemaphoreType.DMA((5,)),
+            pltpu.SemaphoreType.DMA((4,)),
             pltpu.SemaphoreType.DMA,
             pltpu.SemaphoreType.DMA((4, 2)),
             pltpu.SemaphoreType.DMA,

time: 25.1 us -> 25 us (level)
  no operation moved by 1% of the time
where the time goes in v6:
time: 25 us; the launch traced here: 24.9 us
  Pallas kernels  24.2 us (97%)
  other arithmetic  0.63 us (3%)
    pallas_call x1, Pallas kernels, shards(): pl.pallas_call(kernel, out_shape=pltpu.VMEM((2, columns), jnp.float32), i...  24.2 us
    broadcast_in_dim x1, other arithmetic, shards(): return (estimate[0].astype(jnp.float32) - mixed)[None]  0.63 us

profile of v6, /device:TPU:1, one launch (start us, length us, event | category | flops | bytes accessed | tf_op | source)
XLA Modules:
  0.0 24.9 jit_solution(13334390510115650714)
XLA Ops:
  0.0 0.0 copy-start
  0.0 24.2 %shard_map.55 = f32[2,4096]{1,0:T(2,128)S(1)} custom-call(bf16[12,4096]{1,0:T(8,128)(2,1)} %bitcast.8, f32[4,64,128]{2,1,0:T(8,128)} %bitcast.9, s32[1,128]{1,0:T(1,128)} %bitcast.10, f32[3]{0:T(128)} %taps_any.1), custom_call_target="tpu_custom_call" | custom-call | tf_op jit(solution)/shard_map/pallas_call | solution.py:336
  24.2 0.0 copy-done
  24.3 0.6 %fusion = f32[1,2,4096]{2,1,0:T(2,128)} fusion(f32[2,4096]{1,0:T(2,128)S(1)} %shard_map.55, bf16[1,2,4096]{2,1,0:T(2,128)(2,1)S(1)} %copy-done), kind=kLoop, calls=%fused_computation.1 | loop fusion | flops 16384 | bytes 81920 | tf_op jit(solution)/shard_map/broadcast_in_dim | solution.py:362
Async XLA Ops:
  0.0 24.2 %copy-start = (bf16[1,2,4096]{2,1,0:T(2,128)(2,1)S(1)}, bf16[1,2,4096]{2,1,0:T(2,128)(2,1)}, u32[]{:S(2)}) copy-start(bf16[1,2,4096]{2,1,0:T(2,128)(2,1)} %param.6) | copy-start | bytes 49156

commit v7 on v6

--- a/solution.py
+++ b/solution.py
@@ -195,8 +195,14 @@
         natural = 2 * (lax.rem(place, SIDE) * SIDE + z) + lax.rem(col // HALF, 2)
         order = (row == natural).astype(jnp.bfloat16)
         tree = tree_matrix(bank_ref, index_ref) * (1.0 / math.sqrt(views))
+        served = (col == 2 * (lax.rem(row // 2, SIDE) * SIDE + row // (2 * SIDE)) + lax.rem(row, 2)).astype(jnp.bfloat16)
         high, low = [
-            jnp.dot(part, order, preferred_element_type=jnp.float32).astype(jnp.bfloat16) for part in parts_of(tree)
+            jnp.dot(
+                served,
+                jnp.dot(part, order, preferred_element_type=jnp.float32).astype(jnp.bfloat16),
+                preferred_element_type=jnp.float32,
+            ).astype(jnp.bfloat16)
+            for part in parts_of(tree)
         ]
         for part in range(2):
             span = slice(part * GROUPS, (part + 1) * GROUPS)
@@ -217,6 +223,9 @@
                 pl.when(has_side[side])(lambda: wait(HALF))
 
         def merged(part, terms):
+            return jnp.dot(tree_buf[part], terms_of(part, terms), preferred_element_type=jnp.float32)
+
+        def terms_of(part, terms):
             pair = lax.rem(place, SIDE) * (SIDE // 2) + lax.rem(place // SIDE, QUARTER) + part * QUARTER
             moved = [GROUPS // 4 - 1 - pair, pair - GROUPS // 4]
             back = lax.rem(lane - moved[0] + LANES // 2 + LANES, LANES)
@@ -249,23 +258,22 @@
                     )
                 )
             high, low = parts_of(jnp.concatenate(rows, axis=0))
-            return jnp.dot(
-                tree_buf[part], jnp.concatenate([high, high, low], axis=0), preferred_element_type=jnp.float32
-            )
-
-        def keep(e, image):
+            return jnp.concatenate([high, high, low], axis=0)
+
+        def keep(e, image, begin=0):
             for i in range(per_block):
-                result_buf[e, :, i, :] = image[:, i * LANES : (i + 1) * LANES]
+                result_buf[e, begin : begin + image.shape[0], i, :] = image[:, i * LANES : (i + 1) * LANES]
 
         def give(e, step):
             turn = lax.rem(step, SIDE)
             y = jnp.where(turn < SIDE // 2, turn, SIDE + SIDE // 2 - 1 - turn)
-            target = y * SIDE + lax.div(step, SIDE)
+            z = lax.div(step, SIDE)
+            target = y * SIDE + z
 
             @pl.when(jnp.logical_or(target != group, core != e))
             def _():
                 pltpu.make_async_remote_copy(
-                    src_ref=result_buf.at[e, pl.ds(2 * target, 2)],
+                    src_ref=result_buf.at[e, pl.ds(2 * (z * SIDE + y), 2)],
                     dst_ref=image_buf.at[pl.ds(2 * mine, 2)],
                     send_sem=image_send,
                     recv_sem=image_recv.at[mine],
@@ -291,8 +299,17 @@
         give_all(0, AHEAD, (0,))
         early_buf[1] += merged(1, [(0, 1), (1, 2)])
         arrived(3, 1)
-        keep(1, early_buf[1] + merged(1, [(2, 3)]))
-        give_all(0, AHEAD + LEAD, (1,))
+        last = terms_of(1, [(2, 3)])
+        for begin, end in ((0, 2 * SIDE), (2 * SIDE, SIZE)):
+            keep(
+                1,
+                early_buf[1, begin:end]
+                + jnp.dot(tree_buf[1, begin:end], last, preferred_element_type=jnp.float32),
+                begin,
+            )
+            if begin == 0:
+                give_all(0, SIDE, (1,))
+        give_all(SIDE, AHEAD + LEAD, (1,))
 
         def give_both(step, carry):
             give(0, step)
@@ -301,7 +318,7 @@
 
         lax.fori_loop(AHEAD, GROUPS - LEAD, give_both, 0)
         give_all(GROUPS - LEAD, GROUPS, (0,))
-        image_buf[pl.ds(2 * mine, 2)] = result_buf[core, pl.ds(2 * group, 2)]
+        image_buf[pl.ds(2 * mine, 2)] = result_buf[core, pl.ds(2 * (lax.rem(group, SIDE) * SIDE + lax.div(group, SIDE)), 2)]
 
     for b in range(BLOCKS):
         got = image_buf.at[pl.ds(2 * b, 2)]

time: 25 us -> 25 us (level)
  no operation moved by 1% of the time
where the time goes in v7:
time: 25 us; the launch traced here: 24.9 us
  Pallas kernels  24.2 us (97%)
  other arithmetic  0.63 us (3%)
    pallas_call x1, Pallas kernels, shards(): pl.pallas_call(kernel, out_shape=pltpu.VMEM((2, columns), jnp.float32), i...  24.2 us
    broadcast_in_dim x1, other arithmetic, shards(): return (estimate[0].astype(jnp.float32) - mixed)[None]  0.63 us

profile of v7, /device:TPU:1, one launch (start us, length us, event | category | flops | bytes accessed | tf_op | source)
XLA Modules:
  0.0 24.9 jit_solution(9538131430128945758)
XLA Ops:
  0.0 0.0 copy-start
  0.0 24.2 %shard_map.55 = f32[2,4096]{1,0:T(2,128)S(1)} custom-call(bf16[12,4096]{1,0:T(8,128)(2,1)} %bitcast.8, f32[4,64,128]{2,1,0:T(8,128)} %bitcast.9, s32[1,128]{1,0:T(1,128)} %bitcast.10, f32[3]{0:T(128)} %taps_any.1), custom_call_target="tpu_custom_call" | custom-call | tf_op jit(solution)/shard_map/pallas_call | solution.py:353
  24.2 0.0 copy-done
  24.2 0.6 %fusion = f32[1,2,4096]{2,1,0:T(2,128)} fusion(f32[2,4096]{1,0:T(2,128)S(1)} %shard_map.55, bf16[1,2,4096]{2,1,0:T(2,128)(2,1)S(1)} %copy-done), kind=kLoop, calls=%fused_computation.1 | loop fusion | flops 16384 | bytes 81920 | tf_op jit(solution)/shard_map/broadcast_in_dim | solution.py:379
Async XLA Ops:
  0.0 24.2 %copy-start = (bf16[1,2,4096]{2,1,0:T(2,128)(2,1)S(1)}, bf16[1,2,4096]{2,1,0:T(2,128)(2,1)}, u32[]{:S(2)}) copy-start(bf16[1,2,4096]{2,1,0:T(2,128)(2,1)} %param.6) | copy-start | bytes 49156

commit v8 on v7

--- a/solution.py
+++ b/solution.py
@@ -130,15 +130,6 @@
         index_copy.wait()
         taps_copy.wait()
 
-    sino_copy.wait()
-    total = jnp.sum(sino_ref[...].astype(jnp.float32), axis=0, keepdims=True)
-    margin = jnp.zeros((1, LANES // 2), jnp.float32)
-    total = jnp.concatenate([margin, total, margin], axis=1)
-    for b in range(BLOCKS):
-        for c in range(window):
-            start = (b * per_block + c) * LANES
-            send_buf[b, c : c + 1, :] = total[:, start : start + LANES]
-
     has_other = jnp.where(core == 0, cut > 0, cut < slices - 1)
     other_first = lax.rem(jnp.where(core == 0, cut - CORES, cut + 1) + slices, slices)
     other_side = jnp.where(core == 0, 3, 0)
@@ -157,6 +148,15 @@
             device_id=(y * SIDE + z, jnp.where(own, first, other_first) + c),
             device_id_type=MESH,
         )
+
+    sino_copy.wait()
+    total = jnp.sum(sino_ref[...].astype(jnp.float32), axis=0, keepdims=True)
+    margin = jnp.zeros((1, LANES // 2), jnp.float32)
+    total = jnp.concatenate([margin, total, margin], axis=1)
+    for b in range(BLOCKS):
+        for c in range(window):
+            start = (b * per_block + c) * LANES
+            send_buf[b, c : c + 1, :] = total[:, start : start + LANES]
 
     for turn in range(2):
         valid = jnp.where(core != turn, True, has_other)

time: 25 us -> 25 us (level)
  no operation moved by 1% of the time
where the time goes in v8:
time: 25 us; the launch traced here: 24.8 us
  Pallas kernels  24.2 us (97%)
  other arithmetic  0.63 us (3%)
    pallas_call x1, Pallas kernels, shards(): pl.pallas_call(kernel, out_shape=pltpu.VMEM((2, columns), jnp.float32), i...  24.2 us
    broadcast_in_dim x1, other arithmetic, shards(): return (estimate[0].astype(jnp.float32) - mixed)[None]  0.63 us

profile of v8, /device:TPU:1, one launch (start us, length us, event | category | flops | bytes accessed | tf_op | source)
XLA Modules:
  0.0 24.8 jit_solution(5319479409023311116)
XLA Ops:
  0.0 0.0 copy-start
  0.0 24.2 %shard_map.55 = f32[2,4096]{1,0:T(2,128)S(1)} custom-call(bf16[12,4096]{1,0:T(8,128)(2,1)} %bitcast.8, f32[4,64,128]{2,1,0:T(8,128)} %bitcast.9, s32[1,128]{1,0:T(1,128)} %bitcast.10, f32[3]{0:T(128)} %taps_any.1), custom_call_target="tpu_custom_call" | custom-call | tf_op jit(solution)/shard_map/pallas_call | solution.py:353
  24.2 0.0 copy-done
  24.2 0.6 %fusion = f32[1,2,4096]{2,1,0:T(2,128)} fusion(f32[2,4096]{1,0:T(2,128)S(1)} %shard_map.55, bf16[1,2,4096]{2,1,0:T(2,128)(2,1)S(1)} %copy-done), kind=kLoop, calls=%fused_computation.1 | loop fusion | flops 16384 | bytes 81920 | tf_op jit(solution)/shard_map/broadcast_in_dim | solution.py:379
Async XLA Ops:
  0.0 24.2 %copy-start = (bf16[1,2,4096]{2,1,0:T(2,128)(2,1)S(1)}, bf16[1,2,4096]{2,1,0:T(2,128)(2,1)}, u32[]{:S(2)}) copy-start(bf16[1,2,4096]{2,1,0:T(2,128)(2,1)} %param.6) | copy-start | bytes 49156
